TPU v7x, 512 devices: a whole 4x4x16 slice. The times are simulated.
512 devices in a mesh: image: 32 (over z, x_hi), space: 16 (over x_lo, y, core).
Axes of the slice: x: 4 (x_hi: 2, x_lo: 2; x = x_hi * 2 + x_lo), y: 4, z: 16, core: 2. Of those that a mesh axis runs over, the one named last changes fastest.
Arguments:
- positions: float32 [32, 1024, 3, 128], P('image', 'space'), may hold values from 0 to 1
- velocities: float32 [32, 1024, 3, 128], P('image', 'space'), may hold values from -6 to 6
- counts: int32 [1024], P('space'), may hold values from 64 to 128, as said below
- types: int32 [1024, 128], P('space'), may hold values from 0 to 3
- masses: float32 [4], replicated, may hold values from 1 to 16
Outputs:
- positions_out: float32 [32, 1024, 3, 128], P('image', 'space')
- velocities_out: float32 [32, 1024, 3, 128], P('image', 'space')
Inputs may be any that keep to these rules, and one draw needn't show every extreme that they name: `counts`: each cell holds between half of 128 and 128 atoms, and some cell is full.
All inputs are finite; a program needn't handle non-finite values.
Results may differ from a plain program's by a relative error of at most 0.0003.
Values sent between devices are 32-bit elements; how exact they have to be, the bound alone decides.
No kernel may reach another device: no remote copies, remote signals or barrier semaphores. Data moves between devices by JAX's collectives and lax.ppermute only.
A program may use at most 64 MiB of HBM per device.

v0:
```python
import math

import jax
import jax.numpy as jnp
from jax import lax
from jax.sharding import PartitionSpec as P

STEPS = 2


time_step = 1.5
cycle_omega = 6.0
strength = 0.01
width_sq = 0.25


def padded_2(block, sides, width):
    for axis, dim in sides:
        count = lax.axis_size(axis)
        forward = [(i, i + 1) for i in range(count - 1)]
        forward.append((count - 1, 0))
        backward = [(target, source) for source, target in forward]
        low = lax.ppermute(
            lax.slice_in_dim(block, block.shape[dim] - width, None, axis=dim), axis, forward
        )
        high = lax.ppermute(lax.slice_in_dim(block, 0, width, axis=dim), axis, backward)
        block = jnp.concatenate([low, block, high], axis=dim)
    return block


def mode_table(bead_count):
    row_index = lax.broadcasted_iota(jnp.int32, (bead_count, bead_count), 0).astype(jnp.float32)
    col_index = lax.broadcasted_iota(jnp.int32, (bead_count, bead_count), 1).astype(jnp.float32)
    phase_angle = 2.0 * jnp.pi * row_index * col_index / bead_count
    half_count = bead_count // 2
    norm_scale = jnp.sqrt(2.0 / bead_count)
    zero_mode = jnp.ones_like(phase_angle) / jnp.sqrt(float(bead_count))
    middle = jnp.cos(jnp.pi * row_index) / jnp.sqrt(float(bead_count))
    return jnp.where(
        col_index == 0,
        zero_mode,
        jnp.where(
            col_index < half_count,
            norm_scale * jnp.cos(phase_angle),
            jnp.where(col_index == half_count, middle, norm_scale * jnp.sin(phase_angle)),
        ),
    )


def mode_factors(bead_count):
    mode_index = lax.iota(jnp.int32, bead_count).astype(jnp.float32)
    mode_omega = 2.0 * cycle_omega * jnp.sin(jnp.pi * mode_index / bead_count)
    mode_angle = mode_omega * time_step
    cosine = jnp.cos(mode_angle)
    safe_omega = jnp.where(mode_index == 0, 1.0, mode_omega)
    to_velocity = jnp.where(mode_index == 0, 0.0, -mode_omega * jnp.sin(mode_angle))
    to_position = jnp.where(mode_index == 0, time_step, jnp.sin(mode_angle) / safe_omega)
    return (cosine, to_velocity, to_position)


def free_cycle(positions, velocities):
    bead_count = positions.shape[0]
    transform = mode_table(bead_count)
    cosine, to_velocity, to_position = mode_factors(bead_count)
    cosine = cosine[:, None, None, None]
    to_velocity = to_velocity[:, None, None, None]
    to_position = to_position[:, None, None, None]
    mode_pos = jnp.einsum("jk,jcxa->kcxa", transform, positions, precision=lax.Precision.HIGHEST)
    mode_vel = jnp.einsum("jk,jcxa->kcxa", transform, velocities, precision=lax.Precision.HIGHEST)
    next_vel = cosine * mode_vel + to_velocity * mode_pos
    next_pos = to_position * mode_vel + cosine * mode_pos
    new_pos = jnp.einsum("jk,kcxa->jcxa", transform, next_pos, precision=lax.Precision.HIGHEST)
    new_vel = jnp.einsum("jk,kcxa->jcxa", transform, next_vel, precision=lax.Precision.HIGHEST)
    return (new_pos, new_vel)


def cell_force(own_pos, own_mask, near_pos, near_mask):
    offset = (lax.iota(jnp.int32, 3) - 1).astype(jnp.float32)
    diff_x = own_pos[:, None, 0, :, None] - near_pos[:, :, 0, None, :] - offset[None, :, None, None]
    diff_y = own_pos[:, None, 1, :, None] - near_pos[:, :, 1, None, :]
    diff_z = own_pos[:, None, 2, :, None] - near_pos[:, :, 2, None, :]
    weight = (
        strength
        / width_sq
        * jnp.exp(-(diff_x * diff_x + diff_y * diff_y + diff_z * diff_z) / (2.0 * width_sq))
    )
    weight = weight * near_mask[:, :, None, :]
    force_x = jnp.sum(weight * diff_x, axis=(1, 3))
    force_y = jnp.sum(weight * diff_y, axis=(1, 3))
    force_z = jnp.sum(weight * diff_z, axis=(1, 3))
    return jnp.stack([force_x, force_y, force_z], axis=1) * own_mask[:, None, :]


def slab_forces(padded_pos, padded_mask):
    cell_count = padded_pos.shape[0] - 2
    block_cells = math.gcd(8, cell_count)

    def block_force(block_index):
        block_start = block_index * block_cells
        part_pos = lax.dynamic_slice_in_dim(padded_pos, block_start, block_cells + 2, 0)
        part_mask = lax.dynamic_slice_in_dim(padded_mask, block_start, block_cells + 2, 0)
        near_pos = jnp.stack(
            [part_pos[0:block_cells], part_pos[1 : block_cells + 1], part_pos[2:]], axis=1
        )
        near_mask = jnp.stack(
            [part_mask[0:block_cells], part_mask[1 : block_cells + 1], part_mask[2:]], axis=1
        )
        return cell_force(
            part_pos[1 : block_cells + 1], part_mask[1 : block_cells + 1], near_pos, near_mask
        )

    blocked = lax.map(block_force, jnp.arange(cell_count // block_cells, dtype=jnp.int32))
    return blocked.reshape(cell_count, padded_pos.shape[1], padded_pos.shape[2])


def local(positions, velocities, counts, types, masses):
    bead_count = lax.axis_size("image")
    cell_count = positions.shape[1]
    atom_count = positions.shape[3]
    per_group = cell_count // bead_count
    slot_index = lax.broadcasted_iota(jnp.int32, types.shape, 1)
    occupied = (slot_index < counts[:, None]).astype(jnp.float32)
    type_index = lax.broadcasted_iota(jnp.int32, (masses.shape[0],) + types.shape, 0)
    chosen = jnp.sum(jnp.where(types[None] == type_index, masses[:, None, None], 0.0), axis=0)
    inverse_mass = 1.0 / chosen
    kick_scale = 0.5 * time_step * inverse_mass[None, :, None, :]

    def local_forces(bead_field):
        stacked = jnp.concatenate([bead_field, occupied[None, :, None, :]], axis=2)
        padded = padded_2(stacked, (("space", 1),), 1)
        near_field = padded[0, :, 0:3]
        near_mask = padded[0, :, 3]
        return slab_forces(near_field, near_mask)[None]

    forces_now = local_forces(positions)
    for step_index in range(STEPS):
        velocities = velocities + kick_scale * forces_now
        pos_split = positions.reshape(1, bead_count, per_group, 3, atom_count)
        vel_split = velocities.reshape(1, bead_count, per_group, 3, atom_count)
        pos_atoms, vel_atoms = (
            lax.all_to_all(pos_split, "image", split_axis=1, concat_axis=0, tiled=True),
            lax.all_to_all(vel_split, "image", split_axis=1, concat_axis=0, tiled=True),
        )
        pos_cycle, vel_cycle = free_cycle(
            pos_atoms.reshape(bead_count, per_group, 3, atom_count),
            vel_atoms.reshape(bead_count, per_group, 3, atom_count),
        )
        pos_back, vel_back = (
            lax.all_to_all(
                pos_cycle.reshape(bead_count, 1, per_group, 3, atom_count),
                "image",
                split_axis=0,
                concat_axis=1,
                tiled=True,
            ),
            lax.all_to_all(
                vel_cycle.reshape(bead_count, 1, per_group, 3, atom_count),
                "image",
                split_axis=0,
                concat_axis=1,
                tiled=True,
            ),
        )
        positions = pos_back.reshape(1, cell_count, 3, atom_count)
        velocities = vel_back.reshape(1, cell_count, 3, atom_count)
        forces_now = local_forces(positions)
        velocities = velocities + kick_scale * forces_now
    return (positions, velocities)


def solution(mesh):
    return jax.shard_map(
        local,
        mesh=mesh,
        in_specs=(
            P("image", "space", None, None),
            P("image", "space", None, None),
            P("space"),
            P("space", None),
            P(),
        ),
        out_specs=(P("image", "space", None, None), P("image", "space", None, None)),
        check_vma=False,
    )
```

profile of v0, /device:TPU:1, one launch (start us, length us, event | category | flops | bytes accessed | tf_op | source)
XLA Modules:
  0.0 261.7 jit_solution(14427251583410673074)
XLA Ops:
  0.6 1.6 copy.147
  2.2 18.6 %all-to-all-start.1 = ((f32[1,32,2,3,128]{4,2,3,0,1:T(2,128)}), f32[1,32,2,3,128]{4,2,3,0,1:T(2,128)S(1)}, u32[]{:S(2)}, u32[]{:S(2)}) async-start(f32[1,32,2,3,128]{4,2,3,0,1:T(2,128)} %copy.147), calls=%async_computation.1 | async-start | bytes 196608 | tf_op jit(solution)/shard_map/all_to_all | solution.py:141
  21.0 2.9 %collective-permute-start.1 = (f32[1,1,4,128]{3,1,2,0:T(1,128)S(1)}, f32[1,1,4,128]{3,1,2,0:T(1,128)S(1)}, u32[]{:S(2)}, u32[]{:S(2)}) collective-permute-start(f32[1,1,4,128]{3,1,2,0:T(1,128)S(1)} %get-tuple-element.333), channel_id=1, source_target_pairs={{1,0},{2,1},{3,2},{4,3},{5,4},{6,5},{7,6},{8,7},{9,8},{10,9},{11,1... | collective-permute-start | bytes 6152 | tf_op jit(solution)/shard_map/ppermute | solution.py:26
  23.8 3.1 %collective-permute-start = (f32[1,1,4,128]{3,1,2,0:T(1,128)S(1)}, f32[1,1,4,128]{3,1,2,0:T(1,128)S(1)}, u32[]{:S(2)}, u32[]{:S(2)}) collective-permute-start(f32[1,1,4,128]{3,1,2,0:T(1,128)S(1)} %get-tuple-element.289), channel_id=1, source_target_pairs={{0,1},{1,2},{2,3},{3,4},{4,5},{5,6},{6,7},{7,8},{8,9},{9,10},{10,1... | collective-permute-start | bytes 6152 | tf_op jit(solution)/shard_map/ppermute | solution.py:23
  28.7 26.2 %while.36 = (s32[]{:T(128)}, f32[8,8,3,128]{3,1,0,2:T(8,128)S(1)}, s32[8]{0:T(128)S(1)}, f32[66,3,128]{2,0,1:T(8,128)S(1)}, f32[66,128]{1,0:T(8,128)S(1)}, /*ind...) while((s32[]{:T(128)}, f32[8,8,3,128]{3,1,0,2:T(8,128)S(1)}, s32[8]{0:T(128)S(1)}, ...), condition=%wide.region_5.6_spmd, body=%wide.region_1.5_spmd.sunk | while | flops 7111696 | bytes 495903 | solution.py:112
  30.1 1.8 multiply_reduce_fusion.6
  33.4 1.8 multiply_reduce_fusion.6
  36.7 1.8 multiply_reduce_fusion.6
  40.0 1.8 multiply_reduce_fusion.6
  43.3 1.8 multiply_reduce_fusion.6
  46.5 1.8 multiply_reduce_fusion.6
  49.8 1.8 multiply_reduce_fusion.6
  53.1 1.8 multiply_reduce_fusion.6
  55.6 14.6 %all-to-all-start = ((f32[1,32,2,3,128]{4,2,3,0,1:T(2,128)}), f32[1,32,2,3,128]{4,2,3,0,1:T(2,128)S(1)}, u32[]{:S(2)}, u32[]{:S(2)}) async-start(f32[1,32,2,3,128]{4,2,3,0,1:T(2,128)} %copy.144), calls=%async_computation | async-start | bytes 196608 | tf_op jit(solution)/shard_map/all_to_all | solution.py:142
  70.8 13.9 %all-to-all-done = f32[1,32,2,3,128]{4,2,3,0,1:T(2,128)S(1)} async-done(((f32[1,32,2,3,128]{4,2,3,0,1:T(2,128)}), f32[1,32,2,3,128]{4,2,3,0,1:T(2,128)S(1)}, u32[]{:S(2)}, u32[]{:S(2)}) %all-to-all-start) | async-done | bytes 98336 | tf_op jit(solution)/shard_map/all_to_all | solution.py:142
  86.2 4.6 %all-to-all-start.3 = ((f32[32,1,2,3,128]{4,2,3,1,0:T(2,128)}), f32[32,1,2,3,128]{4,2,3,1,0:T(2,128)}, u32[]{:S(2)}, u32[]{:S(2)}) async-start(f32[32,1,2,3,128]{4,2,3,1,0:T(2,128)} %copy.152), calls=%async_computation.3 | async-start | bytes 196608 | tf_op jit(solution)/shard_map/all_to_all | solution.py:149
  90.8 14.3 %all-to-all-done.3 = f32[32,1,2,3,128]{4,2,3,1,0:T(2,128)} async-done(((f32[32,1,2,3,128]{4,2,3,1,0:T(2,128)}), f32[32,1,2,3,128]{4,2,3,1,0:T(2,128)}, u32[]{:S(2)}, u32[]{:S(2)}) %all-to-all-start.3) | async-done | bytes 98336 | tf_op jit(solution)/shard_map/all_to_all | solution.py:149
  106.1 9.0 %collective-permute-start.3 = (f32[1,1,4,128]{3,1,2,0:T(1,128)S(1)}, f32[1,1,4,128]{3,1,2,0:T(1,128)S(1)}, u32[]{:S(2)}, u32[]{:S(2)}) collective-permute-start(f32[1,1,4,128]{3,1,2,0:T(1,128)S(1)} %get-tuple-element.332), channel_id=1, source_target_pairs={{1,0},{2,1},{3,2},{4,3},{5,4},{6,5},{7,6},{8,7},{9,8},{10,9},{11,1... | collective-permute-start | bytes 6152 | tf_op jit(solution)/shard_map/ppermute | solution.py:26
  115.1 1.9 collective-permute-start.2
  118.2 3.9 %all-to-all-start.2 = ((f32[32,1,2,3,128]{4,2,3,1,0:T(2,128)}), f32[32,1,2,3,128]{4,2,3,1,0:T(2,128)S(1)}, u32[]{:S(2)}, u32[]{:S(2)}) async-start(f32[32,1,2,3,128]{4,2,3,1,0:T(2,128)} %copy.150), calls=%async_computation.2 | async-start | bytes 196608 | tf_op jit(solution)/shard_map/all_to_all | solution.py:156
  122.1 14.3 %all-to-all-done.2 = f32[32,1,2,3,128]{4,2,3,1,0:T(2,128)S(1)} async-done(((f32[32,1,2,3,128]{4,2,3,1,0:T(2,128)}), f32[32,1,2,3,128]{4,2,3,1,0:T(2,128)S(1)}, u32[]{:S(2)}, u32[]{:S(2)}) %all-to-all-start.2) | async-done | bytes 98336 | tf_op jit(solution)/shard_map/all_to_all | solution.py:156
  136.5 5.0 %all-to-all-start.5 = ((f32[1,32,2,3,128]{4,2,3,0,1:T(2,128)}), f32[1,32,2,3,128]{4,2,3,0,1:T(2,128)S(1)}, u32[]{:S(2)}, u32[]{:S(2)}) async-start(f32[1,32,2,3,128]{4,2,3,0,1:T(2,128)} %bitcast.72), calls=%async_computation.5 | async-start | bytes 196608 | tf_op jit(solution)/shard_map/all_to_all | solution.py:141
  141.4 26.1 %while.37 = (s32[]{:T(128)}, f32[8,8,3,128]{3,1,0,2:T(8,128)S(1)}, s32[8]{0:T(128)S(1)}, f32[66,3,128]{2,0,1:T(8,128)S(1)}, f32[66,128]{1,0:T(8,128)S(1)}, /*ind...) while((s32[]{:T(128)}, f32[8,8,3,128]{3,1,0,2:T(8,128)S(1)}, s32[8]{0:T(128)S(1)}, ...), condition=%wide.region_10.11_spmd, body=%wide.region_6.10_spmd.sunk | while | flops 7111696 | bytes 495903 | solution.py:112
  142.9 1.8 multiply_reduce_fusion.7
  146.2 1.8 multiply_reduce_fusion.7
  149.4 1.8 multiply_reduce_fusion.7
  152.7 1.8 multiply_reduce_fusion.7
  155.9 1.8 multiply_reduce_fusion.7
  159.2 1.8 multiply_reduce_fusion.7
  162.5 1.8 multiply_reduce_fusion.7
  165.7 1.8 multiply_reduce_fusion.7
  168.3 14.0 %all-to-all-start.4 = ((f32[1,32,2,3,128]{4,2,3,0,1:T(2,128)}), f32[1,32,2,3,128]{4,2,3,0,1:T(2,128)S(1)}, u32[]{:S(2)}, u32[]{:S(2)}) async-start(f32[1,32,2,3,128]{4,2,3,0,1:T(2,128)} %copy.155), calls=%async_computation.4 | async-start | bytes 196608 | tf_op jit(solution)/shard_map/all_to_all | solution.py:142
  182.8 14.0 %all-to-all-done.4 = f32[1,32,2,3,128]{4,2,3,0,1:T(2,128)S(1)} async-done(((f32[1,32,2,3,128]{4,2,3,0,1:T(2,128)}), f32[1,32,2,3,128]{4,2,3,0,1:T(2,128)S(1)}, u32[]{:S(2)}, u32[]{:S(2)}) %all-to-all-start.4) | async-done | bytes 98336 | tf_op jit(solution)/shard_map/all_to_all | solution.py:142
  198.3 3.9 %all-to-all-start.6 = ((f32[32,1,2,3,128]{4,2,3,1,0:T(2,128)}), f32[32,1,2,3,128]{4,2,3,1,0:T(2,128)S(1)}, u32[]{:S(2)}, u32[]{:S(2)}) async-start(f32[32,1,2,3,128]{4,2,3,1,0:T(2,128)} %copy.161), calls=%async_computation.6 | async-start | bytes 196608 | tf_op jit(solution)/shard_map/all_to_all | solution.py:149
  203.2 13.2 %all-to-all-done.6 = f32[32,1,2,3,128]{4,2,3,1,0:T(2,128)S(1)} async-done(((f32[32,1,2,3,128]{4,2,3,1,0:T(2,128)}), f32[32,1,2,3,128]{4,2,3,1,0:T(2,128)S(1)}, u32[]{:S(2)}, u32[]{:S(2)}) %all-to-all-start.6) | async-done | bytes 98336 | tf_op jit(solution)/shard_map/all_to_all | solution.py:149
  216.5 3.9 %all-to-all-start.7 = ((f32[32,1,2,3,128]{4,2,3,1,0:T(2,128)}), f32[32,1,2,3,128]{4,2,3,1,0:T(2,128)S(1)}, u32[]{:S(2)}, u32[]{:S(2)}) async-start(f32[32,1,2,3,128]{4,2,3,1,0:T(2,128)} %copy.163), calls=%async_computation.7 | async-start | bytes 196608 | tf_op jit(solution)/shard_map/all_to_all | solution.py:156
  220.4 6.7 %collective-permute-start.5 = (f32[1,1,4,128]{3,1,2,0:T(1,128)S(1)}, f32[1,1,4,128]{3,1,2,0:T(1,128)S(1)}, u32[]{:S(2)}, u32[]{:S(2)}) collective-permute-start(f32[1,1,4,128]{3,1,2,0:T(1,128)S(1)} %get-tuple-element.330), channel_id=1, source_target_pairs={{1,0},{2,1},{3,2},{4,3},{5,4},{6,5},{7,6},{8,7},{9,8},{10,9},{11,1... | collective-permute-start | bytes 6152 | tf_op jit(solution)/shard_map/ppermute | solution.py:26
  227.1 1.9 collective-permute-start.4
  229.0 5.7 %all-to-all-done.7 = f32[32,1,2,3,128]{4,2,3,1,0:T(2,128)S(1)} async-done(((f32[32,1,2,3,128]{4,2,3,1,0:T(2,128)}), f32[32,1,2,3,128]{4,2,3,1,0:T(2,128)S(1)}, u32[]{:S(2)}, u32[]{:S(2)}) %all-to-all-start.7) | async-done | bytes 98336 | tf_op jit(solution)/shard_map/all_to_all | solution.py:156
  234.8 26.2 %while.38 = (s32[]{:T(128)}, f32[8,8,3,128]{3,1,0,2:T(8,128)S(1)}, s32[8]{0:T(128)S(1)}, f32[66,3,128]{2,0,1:T(8,128)S(1)}, f32[66,128]{1,0:T(8,128)S(1)}, /*ind...) while((s32[]{:T(128)}, f32[8,8,3,128]{3,1,0,2:T(8,128)S(1)}, s32[8]{0:T(128)S(1)}, ...), condition=%wide.region_15.16_spmd, body=%wide.region_11.15_spmd.sunk | while | flops 7111696 | bytes 495903 | solution.py:112
  236.3 1.8 multiply_reduce_fusion.8
  239.6 1.8 multiply_reduce_fusion.8
  242.8 1.8 multiply_reduce_fusion.8
  246.1 1.8 multiply_reduce_fusion.8
  249.4 1.8 multiply_reduce_fusion.8
  252.7 1.8 multiply_reduce_fusion.8
  256.0 1.8 multiply_reduce_fusion.8
  259.2 1.8 multiply_reduce_fusion.8
  (379 shorter events, 28.6 us)
Async XLA Ops:
  0.6 20.2 %copy-start.4 = (s32[64]{0:T(128)S(1)}, s32[64]{0:T(128)}, u32[]{:S(2)}) copy-start(s32[64]{0:T(128)} %param.13) | copy-start | bytes 772
  2.2 18.7 %copy-start = (f32[1,64,3,128]{3,1,2,0:T(8,128)S(1)}, f32[1,64,3,128]{3,1,2,0:T(8,128)}, u32[]{:S(2)}) copy-start(f32[1,64,3,128]{3,1,2,0:T(8,128)} %param.11) | copy-start | bytes 294916
  2.2 24.8 %copy-start.3 = (s32[64,128]{1,0:T(8,128)S(1)}, s32[64,128]{1,0:T(8,128)}, u32[]{:S(2)}) copy-start(s32[64,128]{1,0:T(8,128)} %param.14) | copy-start | bytes 98308
  2.2 24.8 %copy-start.5 = (f32[4]{0:T(128)S(1)}, f32[4]{0:T(128)}, u32[]{:S(2)}) copy-start(f32[4]{0:T(128)} %param.15) | copy-start | bytes 52
  2.2 53.4 %all-to-all-start.1 = ((f32[1,32,2,3,128]{4,2,3,0,1:T(2,128)}), f32[1,32,2,3,128]{4,2,3,0,1:T(2,128)S(1)}, u32[]{:S(2)}, u32[]{:S(2)}) async-start(f32[1,32,2,3,128]{4,2,3,0,1:T(2,128)} %copy.147), calls=%async_computation.1 | async-start | bytes 196608 | tf_op jit(solution)/shard_map/all_to_all | solution.py:141
  21.0 6.2 %collective-permute-start.1 = (f32[1,1,4,128]{3,1,2,0:T(1,128)S(1)}, f32[1,1,4,128]{3,1,2,0:T(1,128)S(1)}, u32[]{:S(2)}, u32[]{:S(2)}) collective-permute-start(f32[1,1,4,128]{3,1,2,0:T(1,128)S(1)} %get-tuple-element.333), channel_id=1, source_target_pairs={{1,0},{2,1},{3,2},{4,3},{5,4},{6,5},{7,6},{8,7},{9,8},{10,9},{11,1... | collective-permute-start | bytes 6152 | tf_op jit(solution)/shard_map/ppermute | solution.py:26
  23.8 4.8 %collective-permute-start = (f32[1,1,4,128]{3,1,2,0:T(1,128)S(1)}, f32[1,1,4,128]{3,1,2,0:T(1,128)S(1)}, u32[]{:S(2)}, u32[]{:S(2)}) collective-permute-start(f32[1,1,4,128]{3,1,2,0:T(1,128)S(1)} %get-tuple-element.289), channel_id=1, source_target_pairs={{0,1},{1,2},{2,3},{3,4},{4,5},{5,6},{6,7},{7,8},{8,9},{9,10},{10,1... | collective-permute-start | bytes 6152 | tf_op jit(solution)/shard_map/ppermute | solution.py:23
  28.7 26.2 %copy-start.2 = (f32[1,64,3,128]{3,1,2,0:T(8,128)S(1)}, f32[1,64,3,128]{3,1,2,0:T(8,128)}, u32[]{:S(2)}) copy-start(f32[1,64,3,128]{3,1,2,0:T(8,128)} %param.12) | copy-start | bytes 294916
  55.6 29.0 %all-to-all-start = ((f32[1,32,2,3,128]{4,2,3,0,1:T(2,128)}), f32[1,32,2,3,128]{4,2,3,0,1:T(2,128)S(1)}, u32[]{:S(2)}, u32[]{:S(2)}) async-start(f32[1,32,2,3,128]{4,2,3,0,1:T(2,128)} %copy.144), calls=%async_computation | async-start | bytes 196608 | tf_op jit(solution)/shard_map/all_to_all | solution.py:142
  86.2 19.0 %all-to-all-start.3 = ((f32[32,1,2,3,128]{4,2,3,1,0:T(2,128)}), f32[32,1,2,3,128]{4,2,3,1,0:T(2,128)}, u32[]{:S(2)}, u32[]{:S(2)}) async-start(f32[32,1,2,3,128]{4,2,3,1,0:T(2,128)} %copy.152), calls=%async_computation.3 | async-start | bytes 196608 | tf_op jit(solution)/shard_map/all_to_all | solution.py:149
  106.1 15.9 %collective-permute-start.3 = (f32[1,1,4,128]{3,1,2,0:T(1,128)S(1)}, f32[1,1,4,128]{3,1,2,0:T(1,128)S(1)}, u32[]{:S(2)}, u32[]{:S(2)}) collective-permute-start(f32[1,1,4,128]{3,1,2,0:T(1,128)S(1)} %get-tuple-element.332), channel_id=1, source_target_pairs={{1,0},{2,1},{3,2},{4,3},{5,4},{6,5},{7,6},{8,7},{9,8},{10,9},{11,1... | collective-permute-start | bytes 6152 | tf_op jit(solution)/shard_map/ppermute | solution.py:26
  115.1 6.9 %collective-permute-start.2 = (f32[1,1,4,128]{3,1,2,0:T(1,128)S(1)}, f32[1,1,4,128]{3,1,2,0:T(1,128)S(1)}, u32[]{:S(2)}, u32[]{:S(2)}) collective-permute-start(f32[1,1,4,128]{3,1,2,0:T(1,128)S(1)} %get-tuple-element.331), channel_id=1, source_target_pairs={{0,1},{1,2},{2,3},{3,4},{4,5},{5,6},{6,7},{7,8},{8,9},{9,10},{10,1... | collective-permute-start | bytes 6152 | tf_op jit(solution)/shard_map/ppermute | solution.py:23
  118.2 18.3 %all-to-all-start.2 = ((f32[32,1,2,3,128]{4,2,3,1,0:T(2,128)}), f32[32,1,2,3,128]{4,2,3,1,0:T(2,128)S(1)}, u32[]{:S(2)}, u32[]{:S(2)}) async-start(f32[32,1,2,3,128]{4,2,3,1,0:T(2,128)} %copy.150), calls=%async_computation.2 | async-start | bytes 196608 | tf_op jit(solution)/shard_map/all_to_all | solution.py:156
  136.5 31.8 %all-to-all-start.5 = ((f32[1,32,2,3,128]{4,2,3,0,1:T(2,128)}), f32[1,32,2,3,128]{4,2,3,0,1:T(2,128)S(1)}, u32[]{:S(2)}, u32[]{:S(2)}) async-start(f32[1,32,2,3,128]{4,2,3,0,1:T(2,128)} %bitcast.72), calls=%async_computation.5 | async-start | bytes 196608 | tf_op jit(solution)/shard_map/all_to_all | solution.py:141
  168.3 28.4 %all-to-all-start.4 = ((f32[1,32,2,3,128]{4,2,3,0,1:T(2,128)}), f32[1,32,2,3,128]{4,2,3,0,1:T(2,128)S(1)}, u32[]{:S(2)}, u32[]{:S(2)}) async-start(f32[1,32,2,3,128]{4,2,3,0,1:T(2,128)} %copy.155), calls=%async_computation.4 | async-start | bytes 196608 | tf_op jit(solution)/shard_map/all_to_all | solution.py:142
  198.3 18.2 %all-to-all-start.6 = ((f32[32,1,2,3,128]{4,2,3,1,0:T(2,128)}), f32[32,1,2,3,128]{4,2,3,1,0:T(2,128)S(1)}, u32[]{:S(2)}, u32[]{:S(2)}) async-start(f32[32,1,2,3,128]{4,2,3,1,0:T(2,128)} %copy.161), calls=%async_computation.6 | async-start | bytes 196608 | tf_op jit(solution)/shard_map/all_to_all | solution.py:149
  216.5 18.2 %all-to-all-start.7 = ((f32[32,1,2,3,128]{4,2,3,1,0:T(2,128)}), f32[32,1,2,3,128]{4,2,3,1,0:T(2,128)S(1)}, u32[]{:S(2)}, u32[]{:S(2)}) async-start(f32[32,1,2,3,128]{4,2,3,1,0:T(2,128)} %copy.163), calls=%async_computation.7 | async-start | bytes 196608 | tf_op jit(solution)/shard_map/all_to_all | solution.py:156
  220.4 14.4 %copy-start.1 = (f32[32,1,2,3,128]{4,2,0,3,1:T(2,128)}, f32[32,1,2,3,128]{4,2,0,3,1:T(2,128)S(1)}, u32[]{:S(2)}) copy-start(f32[32,1,2,3,128]{4,2,0,3,1:T(2,128)S(1)} %copy.162) | copy-start | bytes 294916
  220.4 14.3 %collective-permute-start.5 = (f32[1,1,4,128]{3,1,2,0:T(1,128)S(1)}, f32[1,1,4,128]{3,1,2,0:T(1,128)S(1)}, u32[]{:S(2)}, u32[]{:S(2)}) collective-permute-start(f32[1,1,4,128]{3,1,2,0:T(1,128)S(1)} %get-tuple-element.330), channel_id=1, source_target_pairs={{1,0},{2,1},{3,2},{4,3},{5,4},{6,5},{7,6},{8,7},{9,8},{10,9},{11,1... | collective-permute-start | bytes 6152 | tf_op jit(solution)/shard_map/ppermute | solution.py:26
  227.1 7.7 %collective-permute-start.4 = (f32[1,1,4,128]{3,1,2,0:T(1,128)S(1)}, f32[1,1,4,128]{3,1,2,0:T(1,128)S(1)}, u32[]{:S(2)}, u32[]{:S(2)}) collective-permute-start(f32[1,1,4,128]{3,1,2,0:T(1,128)S(1)} %get-tuple-element.329), channel_id=1, source_target_pairs={{0,1},{1,2},{2,3},{3,4},{4,5},{5,6},{6,7},{7,8},{8,9},{9,10},{10,1... | collective-permute-start | bytes 6152 | tf_op jit(solution)/shard_map/ppermute | solution.py:23
where the time goes:
time: 266 us; the launch traced here: 262 us
  starting transfers between devices  93.9 us (35%)
  waiting for transfers between devices  76.9 us (29%)
  other arithmetic  44.6 us (17%)
  local copies, waits for them, and re-layouts  23.7 us (9%)
  loops' own time  18.3 us (7%)
  matrix products  3.17 us (1%)
    reduce_sum x24, other arithmetic, cell_force(): force_x = jnp.sum(weight * diff_x, axis=(1, 3))  42.8 us
    all_to_all x2, starting transfers between devices, local(): lax.all_to_all(vel_split, 'image', split_axis=1, concat_axis=0, tiled=True)  28.6 us
    all_to_all x2, waiting for transfers between devices, local(): lax.all_to_all(vel_split, 'image', split_axis=1, concat_axis=0, tiled=True)  27.9 us
    all_to_all x2, waiting for transfers between devices, local(): lax.all_to_all(pos_cycle.reshape(bead_count, 1, per_group, 3, atom_count)...  27.6 us
    all_to_all x2, starting transfers between devices, local(): lax.all_to_all(pos_split, 'image', split_axis=1, concat_axis=0, tiled=True)  23.6 us
    all_to_all x2, waiting for transfers between devices, local(): lax.all_to_all(vel_cycle.reshape(bead_count, 1, per_group, 3, atom_count)...  20 us
    ppermute x3, starting transfers between devices, padded_2(): lax.ppermute(lax.slice_in_dim(block, 0, width, axis=dim), axis, backward)  18.6 us
    another operation x3, loops' own time, slab_forces(): lax.map(block_force, jnp.arange(cell_count // block_cells, dtype=jnp.int32))  18.3 us
  transfers between devices with their start and end apart: 14, of which 7 were waited for; matrix products, arithmetic and copies ran while one was open for 17% of the time, Pallas kernels for 0%

commit v1 on v0

v1 whole, which is shorter than its diff:
```python
import math

import jax
import jax.numpy as jnp
import numpy as np
from jax import lax
from jax.experimental import pallas as pl
from jax.experimental.pallas import tpu as pltpu
from jax.sharding import PartitionSpec as P

STEPS = 2

time_step = 1.5
cycle_omega = 6.0
strength = 0.01
width_sq = 0.25

F32 = jnp.float32
BF16 = jnp.bfloat16
LANES = 128
ROWS = 24
SPAN = 12
ALPHA = math.sqrt(math.log2(math.e) / width_sq)
GAIN = strength / width_sq / ALPHA
FAR = 1e12


def cycle_matrix(count):
    j = np.arange(count, dtype=np.float64)[:, None]
    k = np.arange(count, dtype=np.float64)[None, :]
    half = count // 2
    phase = 2.0 * np.pi * j * k / count
    table = np.where(
        k < half, np.sqrt(2.0 / count) * np.cos(phase), np.sqrt(2.0 / count) * np.sin(phase)
    )
    table = np.where(k == 0, 1.0 / np.sqrt(count), table)
    table = np.where(k == half, np.cos(np.pi * j) / np.sqrt(count), table)
    omega = 2.0 * cycle_omega * np.sin(np.pi * k[0] / count)
    angle = omega * time_step
    to_position = np.where(k[0] == 0, time_step, np.sin(angle) / np.where(k[0] == 0, 1.0, omega))
    same = (table * np.cos(angle)) @ table.T
    from_velocity = (table * to_position) @ table.T
    from_position = (table * (-omega * np.sin(angle))) @ table.T
    return np.block([[same, from_velocity], [from_position, same]]).astype(np.float32)


def split3(value):
    high = value.astype(BF16).astype(F32)
    rest = value - high
    mid = rest.astype(BF16).astype(F32)
    low = (rest - mid).astype(BF16).astype(F32)
    return high, mid, low


def put_tables(planes, occupied, tables, start, stride=1):
    left, right, moved = tables
    count = planes[0].shape[0]
    one = jnp.ones_like(planes[0])

    def put(ref, row, value):
        ref[pl.ds(start * ROWS + row, count, stride=stride * ROWS), :] = value

    def norm(parts):
        total = parts[0] * parts[0] + parts[1] * parts[1] + parts[2] * parts[2]
        return split3(-0.5 * total - FAR * (1.0 - occupied))

    scaled = [ALPHA * plane for plane in planes]
    pieces = [split3(part) for part in scaled]
    norms = norm(scaled)
    for axis in range(3):
        high, mid, low = pieces[axis]
        for row, value in ((0, high), (4, mid), (8, high), (12, low), (16, high), (20, mid)):
            put(left, row + axis, value)
        for row, value in ((0, high), (4, high), (8, mid), (12, high), (16, low), (20, mid)):
            put(right, row + axis, value)
            if axis:
                put(moved, row + axis, value)
    for piece in range(3):
        put(left, 8 * piece + 3, norms[piece])
        put(left, 8 * piece + 7, one)
        put(right, 8 * piece + 3, one)
        put(right, 8 * piece + 7, norms[piece])
        put(moved, 8 * piece + 3, one)
    ahead = ALPHA * (planes[0] + 1.0)
    high, mid, low = split3(ahead)
    for row, value in ((0, high), (4, high), (8, mid), (12, high), (16, low), (20, mid)):
        put(moved, row, value)
    norms = norm([ahead, scaled[1], scaled[2]])
    for piece in range(3):
        put(moved, 8 * piece + 7, norms[piece])


def fold(sums):
    return sums[0:8], sums[0:8] + sums[8:16] + sums[16:24]


def pair_sums(tables, own, near):
    left, right, moved = tables
    pad = jnp.zeros((8, LANES), F32)

    def rows(ref, cell):
        return ref[pl.ds(pl.multiple_of(cell * ROWS, 8), ROWS), :]

    table = rows(right, own)
    place = table[0:8] + table[8:16] + table[16:24]
    left_rows = jnp.concatenate([rows(left, own), pad], axis=0).astype(BF16)
    own_rows = jnp.concatenate([table, pad], axis=0).astype(BF16)
    near_rows = jnp.concatenate([rows(moved, near), pad], axis=0).astype(BF16)
    both = jnp.concatenate([own_rows, near_rows], axis=1)
    exponent = lax.dot_general(
        left_rows, both, (((0,), (0,)), ((), ())), preferred_element_type=F32
    )
    weight = jnp.exp2(exponent).astype(BF16)
    to_own = lax.dot_general(
        both, weight, (((1,), (1,)), ((), ())), preferred_element_type=F32
    )
    to_near = lax.dot_general(
        own_rows, weight[:, LANES:], (((1,), (0,)), ((), ())), preferred_element_type=F32
    )
    return place, fold(to_own), fold(to_near)


def force_of(place, sums, carry):
    shift = jnp.where(lax.broadcasted_iota(jnp.int32, (8, LANES), 0) == 0, ALPHA, 0.0)
    from_right = place * sums[0][3:4] - sums[1]
    from_left = (place + shift) * carry[0][3:4] - carry[1]
    return GAIN * (from_right + from_left)


def chain_forces(tables, count, emit):
    zero = jnp.zeros((8, LANES), F32)
    unroll = next(u for u in (5, 3, 1) if (count - 1) % u == 0)

    def body(step, carry):
        for part in range(unroll):
            cell = step * unroll + part
            place, sums, onward = pair_sums(tables, cell, cell + 1)
            emit(cell, force_of(place, sums, carry))
            carry = onward
        return carry

    lax.fori_loop(0, (count - 1) // unroll, body, (zero, zero))


def scratch(rows):
    return pltpu.VMEM((rows, LANES), F32)


VMEM = pl.BlockSpec(memory_space=pltpu.VMEM)
PARAMS = pltpu.CompilerParams(vmem_limit_bytes=48 * 1024 * 1024)


def edge_kernel(cells, pos_ref, vel_ref, occ_ref, kick_ref, out_ref):
    for axis in range(3):
        out_ref[axis : axis + 1, :] = pos_ref[axis, cells - 2 : cells - 1, :]
        out_ref[3 + axis : 4 + axis, :] = pos_ref[axis, cells - 1 : cells, :]
        out_ref[6 + axis : 7 + axis, :] = vel_ref[axis, cells - 1 : cells, :]
    out_ref[9:11, :] = occ_ref[cells - 2 : cells, :]
    out_ref[11:12, :] = kick_ref[cells - 1 : cells, :]
    out_ref[12:16, :] = jnp.zeros((4, LANES), F32)


def first_kernel(
    cells, edge_ref, pos_ref, vel_ref, occ_ref, kick_ref, send_ref,
    place, speed, occ_all, left, right, moved,
):
    half = cells // 4
    place[0:3, :] = edge_ref[0:3, :]
    place[8:11, :] = edge_ref[3:6, :]
    speed[8:11, :] = edge_ref[6:9, :]
    place[11:12, :] = edge_ref[11:12, :]
    for axis in range(3):
        place[pl.ds(2 * 8 + axis, cells, stride=8), :] = pos_ref[axis]
        speed[pl.ds(2 * 8 + axis, cells, stride=8), :] = vel_ref[axis]
    place[pl.ds(2 * 8 + 3, cells, stride=8), :] = kick_ref[...]
    occ_all[0:2, :] = edge_ref[9:11, :]
    occ_all[2 : cells + 2, :] = occ_ref[...]
    tables = (left, right, moved)
    count = cells + 8
    planes = [place[pl.ds(axis, count, stride=8), :] for axis in range(3)]
    put_tables(planes, occ_all[...], tables, 0)

    def emit(slot, force):
        rows = pl.ds(pl.multiple_of(slot * 8, 8), 8)
        kick = place[rows, :][3:4]
        speed[rows, :] = speed[rows, :] + kick * force

    chain_forces(tables, cells + 2, emit)
    for kind, source in enumerate((place, speed)):
        for axis in range(3):
            for parity in range(2):
                row = (kind * 3 + axis) * 2 + parity
                for part in range(2):
                    first = (part * 2 * half + 1 + parity) * 8 + axis
                    send_ref[pl.ds(part * SPAN + row, half, stride=2 * SPAN), :] = source[
                        pl.ds(first, half, stride=16), :
                    ]


def cycle(matrix_ref, blocks):
    return jnp.dot(
        matrix_ref[...],
        jnp.concatenate(blocks, axis=1),
        precision=lax.Precision.HIGHEST,
        preferred_element_type=F32,
    )


def turn_kernel(images, matrix_ref, got_ref, low_ref, high_ref, vel_ref):
    blocks = []
    for parity in range(2):
        for axis in range(3):
            parts = [
                got_ref[pl.ds((kind * 3 + axis) * 2 + parity, images, stride=SPAN), :]
                for kind in range(2)
            ]
            blocks.append(jnp.concatenate(parts, axis=0))
    ahead = cycle(matrix_ref, blocks)
    for parity, out_ref in enumerate((low_ref, high_ref)):
        for axis in range(3):
            index = parity * 3 + axis
            lanes = slice(index * LANES, (index + 1) * LANES)
            out_ref[axis * images : (axis + 1) * images, :] = ahead[:images, lanes]
            vel_ref[index * images : (index + 1) * images, :] = ahead[images:, lanes]


def middle_kernel(
    images, matrix_ref, info_ref, before_ref, low_ref, high_ref, after_ref, vel_ref, send_ref,
    forces, left, right, moved,
):
    tables = (left, right, moved)
    for slot, ref in enumerate((before_ref, low_ref, high_ref, after_ref)):
        planes = [ref[axis * images : (axis + 1) * images, :] for axis in range(3)]
        occupied = jnp.broadcast_to(info_ref[slot : slot + 1, :], (images, LANES))
        put_tables(planes, occupied, tables, slot, stride=4)

    def body(image, _):
        first = image * 4
        place, sums, carry = pair_sums(tables, first, first + 1)
        for parity in range(2):
            place, sums, onward = pair_sums(tables, first + 1 + parity, first + 2 + parity)
            rows = pl.ds(pl.multiple_of((image * 2 + parity) * 8, 8), 8)
            forces[rows, :] = force_of(place, sums, carry)
            carry = onward
        return 0

    def two(step, _):
        body(step * 2, 0)
        body(step * 2 + 1, 0)
        return 0

    lax.fori_loop(0, images // 2, two, 0)
    blocks = []
    for parity, ref in enumerate((low_ref, high_ref)):
        kick = 2.0 * info_ref[4 + parity : 5 + parity, :]
        for axis in range(3):
            index = parity * 3 + axis
            force = forces[pl.ds(parity * 8 + axis, images, stride=16), :]
            speed = vel_ref[index * images : (index + 1) * images, :] + kick * force
            blocks.append(
                jnp.concatenate([ref[axis * images : (axis + 1) * images, :], speed], axis=0)
            )
    ahead = cycle(matrix_ref, blocks)
    for parity in range(2):
        for axis in range(3):
            index = parity * 3 + axis
            lanes = slice(index * LANES, (index + 1) * LANES)
            for kind in range(2):
                row = (kind * 3 + axis) * 2 + parity
                send_ref[pl.ds(row, images, stride=SPAN), :] = ahead[
                    kind * images : (kind + 1) * images, lanes
                ]


def last_kernel(
    cells, got_ref, edge_ref, first_ref, occ_ref, kick_ref, pos_ref, vel_ref,
    place, speed, occ_all, left, right, moved,
):
    half = cells // 4
    for kind, target in enumerate((place, speed)):
        for axis in range(3):
            for parity in range(2):
                row = (kind * 3 + axis) * 2 + parity
                for part in range(2):
                    first = (part * 2 * half + parity) * 8 + axis
                    target[pl.ds(first, half, stride=16), :] = got_ref[
                        pl.ds(part * SPAN + row, half, stride=2 * SPAN), :
                    ]
                if kind == 0 or parity == 0:
                    slot = (cells + parity) * 8 + axis
                    target[slot : slot + 1, :] = edge_ref[row : row + 1, :]
    place[pl.ds(8 + 3, cells, stride=8), :] = kick_ref[...]
    occ_all[0:1, :] = first_ref[10:11, :]
    occ_all[1 : cells + 1, :] = occ_ref[...]
    occ_all[cells + 1 : cells + 2, :] = edge_ref[12:13, :]
    tables = (left, right, moved)
    count = cells + 8
    planes = [place[pl.ds(axis, count, stride=8), :] for axis in range(3)]
    put_tables(planes, occ_all[...], tables, 0)

    def emit(slot, force):
        rows = pl.ds(pl.multiple_of(slot * 8, 8), 8)
        kick = place[rows, :][3:4]
        speed[rows, :] = speed[rows, :] + kick * force

    chain_forces(tables, cells + 2, emit)
    for axis in range(3):
        pos_ref[axis] = place[pl.ds(8 + axis, cells, stride=8), :]
        vel_ref[axis] = speed[pl.ds(8 + axis, cells, stride=8), :]


def local(positions, velocities, counts, types, masses):
    images = lax.axis_size("image")
    slabs = lax.axis_size("space")
    cells = positions.shape[1]
    rows = cells + 8
    place_of = lambda block: 2 * (block % (images // 2)) + block // (images // 2)

    def device(block):
        block %= images * slabs
        slab, inside = divmod(block, images)
        return place_of(inside) * slabs + slab

    def shift(array, distance):
        pairs = [(device(b), device(b + distance)) for b in range(images * slabs)]
        return lax.ppermute(array, ("image", "space"), pairs)

    def slab_shift(array, distance):
        pairs = [(s, (s + distance) % slabs) for s in range(slabs)]
        return lax.ppermute(array, "space", pairs)

    def transpose(array):
        blocks = array.reshape(images, SPAN // 4, 4, LANES)
        blocks = lax.all_to_all(blocks, "image", split_axis=0, concat_axis=0, tiled=True)
        return blocks.reshape(array.shape)

    def call(kernel, outs, scratches, *args):
        return pl.pallas_call(
            kernel,
            out_shape=outs,
            in_specs=[VMEM] * len(args),
            out_specs=jax.tree.map(lambda _: VMEM, outs),
            scratch_shapes=scratches,
            compiler_params=PARAMS,
        )(*args)

    def shaped(*shape):
        return jax.ShapeDtypeStruct(shape, F32)

    slot_index = lax.broadcasted_iota(jnp.int32, types.shape, 1)
    occupied = (slot_index < counts[:, None]).astype(F32)
    type_index = lax.broadcasted_iota(jnp.int32, (masses.shape[0],) + types.shape, 0)
    chosen = jnp.sum(jnp.where(types[None] == type_index, masses[:, None, None], 0.0), axis=0)
    kick = 0.5 * time_step * (1.0 / chosen)
    matrix = jnp.asarray(cycle_matrix(images))
    group = lax.axis_index("image")
    block = (group % 2) * (images // 2) + group // 2

    pos = positions[0].transpose(1, 0, 2)
    vel = velocities[0].transpose(1, 0, 2)
    cell_tables = [scratch(rows * ROWS)] * 3
    edge = call(lambda *r: edge_kernel(cells, *r), shaped(16, LANES), [], pos, vel, occupied, kick)
    edge = slab_shift(edge, 1)
    send = call(
        lambda *r: first_kernel(cells, *r),
        shaped(images * SPAN, LANES),
        [scratch(rows * 8), scratch(rows * 8), scratch(rows)] + cell_tables,
        edge, pos, vel, occupied, kick,
    )
    got = transpose(send)
    low, high, speed = call(
        lambda *r: turn_kernel(images, *r),
        (shaped(3 * images, LANES), shaped(3 * images, LANES), shaped(6 * images, LANES)),
        [],
        matrix, got,
    )
    before = shift(high, 1)
    after = shift(low, -1)
    occ_wide = jnp.concatenate([edge[9:11], occupied], axis=0)
    kick_wide = jnp.concatenate([edge[11:12], kick], axis=0)
    info = jnp.concatenate(
        [
            lax.dynamic_slice_in_dim(occ_wide, 2 * block, 4, 0),
            lax.dynamic_slice_in_dim(kick_wide, 2 * block, 2, 0),
            jnp.zeros((2, LANES), F32),
        ],
        axis=0,
    )
    send = call(
        lambda *r: middle_kernel(images, *r),
        shaped(images * SPAN, LANES),
        [scratch(2 * images * 8)] + [scratch(4 * images * ROWS)] * 3,
        matrix, info, before, low, high, after, speed,
    )
    got = transpose(send)
    message = jnp.concatenate([got[0:SPAN], occupied[0:1], jnp.zeros((3, LANES), F32)], axis=0)
    message = slab_shift(message, -1)
    pos, vel = call(
        lambda *r: last_kernel(cells, *r),
        (shaped(*pos.shape), shaped(*vel.shape)),
        [scratch(rows * 8), scratch(rows * 8), scratch(rows)] + cell_tables,
        got, message, edge, occupied, kick,
    )
    return pos.transpose(1, 0, 2)[None], vel.transpose(1, 0, 2)[None]


def solution(mesh):
    return jax.shard_map(
        local,
        mesh=mesh,
        in_specs=(
            P("image", "space", None, None),
            P("image", "space", None, None),
            P("space"),
            P("space", None),
            P(),
        ),
        out_specs=(P("image", "space", None, None), P("image", "space", None, None)),
        check_vma=False,
    )
```

time: 266 us -> 137 us (0.52); the launches traced: 262 us -> 137 us
  starting transfers between devices: 93.9 us -> 43.6 us
  Pallas kernels: 0 us -> 46.2 us
  other arithmetic: 44.6 us -> 1.04 us
  waiting for transfers between devices: 76.9 us -> 43.1 us
  local copies, waits for them, and re-layouts: 23.7 us -> 1.75 us
  loops' own time: 18.3 us -> 0 us
  matrix products: 3.17 us -> 0 us
    pallas_call x0 -> x5, Pallas kernels: none -> 46.2 us  [call(): pl.pallas_call(kernel, out_shape=outs, in_specs=[VMEM] * len(args), out_s...]
    reduce_sum x24 -> x0, other arithmetic: 42.8 us -> none  [cell_force(): force_x = jnp.sum(weight * diff_x, axis=(1, 3))]
    all_to_all x8 -> x2, starting transfers between devices: 68.4 us -> 26.1 us  [transpose(): lax.all_to_all(blocks, 'image', split_axis=0, concat_axis=0, tiled=True)]
    all_to_all x8 -> x2, waiting for transfers between devices: 75.4 us -> 34.6 us  [transpose(): lax.all_to_all(blocks, 'image', split_axis=0, concat_axis=0, tiled=True)]
    another operation x3 -> x0, loops' own time: 18.3 us -> none  [slab_forces(): lax.map(block_force, jnp.arange(cell_count // block_cells, dtype=jnp.int32))]
    dynamic_slice x24 -> x0, local copies, waits for them, and re-layouts: 14.7 us -> none  [slab_forces(): lax.map(block_force, jnp.arange(cell_count // block_cells, dtype=jnp.int32))]
    ppermute x6 -> x4, starting transfers between devices: 25.5 us -> 17.5 us  [the longest x2 10.5 us: shift(): return lax.ppermute(array, ('image', 'space'), pairs)]
    ppermute x6 -> x4, waiting for transfers between devices: 1.45 us -> 8.59 us  [the longest x2 7.5 us: slab_shift(): return lax.ppermute(array, 'space', pairs)]
  transfers between devices with their start and end apart: 14 -> 6, of which waited for: 7 -> 5; matrix products, arithmetic and copies ran while one was open for 17% -> 0% of each run, Pallas kernels for 0% -> 0%
where the time goes in v1:
time: 137 us
  Pallas kernels  46.2 us (34%)
  starting transfers between devices  43.6 us (32%)
  waiting for transfers between devices  43.1 us (31%)
  local copies, waits for them, and re-layouts  1.75 us (1%)
    pallas_call x5, Pallas kernels, call(): pl.pallas_call(kernel, out_shape=outs, in_specs=[VMEM] * len(args), out_s...  46.2 us
    all_to_all x2, waiting for transfers between devices, transpose(): lax.all_to_all(blocks, 'image', split_axis=0, concat_axis=0, tiled=True)  34.6 us
    all_to_all x2, starting transfers between devices, transpose(): lax.all_to_all(blocks, 'image', split_axis=0, concat_axis=0, tiled=True)  26.1 us
    ppermute x2, starting transfers between devices, shift(): return lax.ppermute(array, ('image', 'space'), pairs)  10.5 us
    ppermute x2, waiting for transfers between devices, slab_shift(): return lax.ppermute(array, 'space', pairs)  7.5 us
    ppermute x2, starting transfers between devices, slab_shift(): return lax.ppermute(array, 'space', pairs)  7.02 us
  transfers between devices with their start and end apart: 6, of which 5 were waited for; matrix products, arithmetic and copies ran while one was open for 0% of the time, Pallas kernels for 0%

profile of v1, /device:TPU:1, one launch (start us, length us, event | category | flops | bytes accessed | tf_op | source)
XLA Modules:
  0.0 136.6 jit_solution(2448406507094700112)
XLA Ops:
  0.6 0.0 copy-start.7
  0.6 0.0 copy-start.6
  0.7 0.0 copy-start.2
  0.7 0.8 fusion.r_2_.r_3_
  1.4 0.0 copy-done.7
  1.4 0.0 copy-done.6
  1.4 0.0 copy-start
  1.5 0.1 select_reduce_fusion
  1.6 0.0 copy-done.2
  1.6 0.0 copy-start.3
  1.6 0.9 copy-done.3
  2.5 0.0 copy-start.4
  2.5 4.7 %collective-permute-start = (f32[16,128]{1,0:T(8,128)S(1)}, f32[16,128]{1,0:T(8,128)S(1)}, u32[]{:S(2)}, u32[]{:S(2)}) collective-permute-start(f32[16,128]{1,0:T(8,128)S(1)} %shard_map.77), channel_id=1, source_target_pairs={{0,1},{1,2},{2,3},{3,4},{4,5},{5,6},{6,7},{7,8},{8,9},{9,10},{10,1... | collective-permute-start | bytes 24584 | tf_op jit(solution)/shard_map/ppermute | solution.py:330
  7.2 4.8 %collective-permute-done.r_0_.r_2_ = f32[16,128]{1,0:T(8,128)S(1)} collective-permute-done((f32[16,128]{1,0:T(8,128)S(1)}, f32[16,128]{1,0:T(8,128)S(1)}, u32[]{:S(2)}, u32[]{:S(2)}) %collective-permute-start) | collective-permute-done | bytes 8224 | tf_op jit(solution)/shard_map/ppermute | solution.py:330
  12.1 0.0 copy-done.4
  12.1 14.5 %shard_map.78 = f32[384,128]{1,0:T(8,128)} custom-call(f32[16,128]{1,0:T(8,128)S(1)} %collective-permute-done.r_0_.r_2_, f32[3,64,128]{2,1,0:T(8,128)S(1)} %bitcast.19, f32[3,64,128]{2,1,0:T(8,128)S(1)} %bitcast.21, f32[64,128]{1,0:T(8,128)S(1)} %fusion.r_2_.r_3_, f32[64,128]{1,0:T(8,128)S(1)} %divide_multiply_fusion.r_3_.r_4_), custom_call_target="tpu_custom_call" | custom-call | tf_op jit(solution)/shard_map/pallas_call | solution.py:338
  26.5 13.6 %all-to-all-start = ((f32[32,3,4,128]{3,2,1,0:T(4,128)}), f32[32,3,4,128]{3,2,1,0:T(4,128)S(1)}, u32[]{:S(2)}, u32[]{:S(2)}) async-start(f32[32,3,4,128]{3,2,1,0:T(4,128)} %bitcast.6), calls=%async_computation | async-start | bytes 393216 | tf_op jit(solution)/shard_map/all_to_all | solution.py:334
  40.2 0.1 pad.5.clone
  40.2 0.0 copy-start.5
  40.3 15.3 %all-to-all-done = f32[32,3,4,128]{3,2,1,0:T(4,128)S(1)} async-done(((f32[32,3,4,128]{3,2,1,0:T(4,128)}), f32[32,3,4,128]{3,2,1,0:T(4,128)S(1)}, u32[]{:S(2)}, u32[]{:S(2)}) %all-to-all-start) | async-done | bytes 196640 | tf_op jit(solution)/shard_map/all_to_all | solution.py:334
  55.6 0.0 copy-done.5
  55.6 0.3 shard_map.79
  55.9 2.1 %collective-permute-start.1 = (f32[96,128]{1,0:T(8,128)S(1)}, f32[96,128]{1,0:T(8,128)S(1)}, u32[]{:S(2)}, u32[]{:S(2)}) collective-permute-start(f32[96,128]{1,0:T(8,128)S(1)} %get-tuple-element.7.r_4_), channel_id=1, source_target_pairs={{0,32},{32,64},{64,96},{96,128},{128,160},{160,192},{192,224},{224... | collective-permute-start | bytes 147464 | tf_op jit(solution)/shard_map/ppermute | solution.py:326
  58.0 8.4 %collective-permute-start.2 = (f32[96,128]{1,0:T(8,128)S(1)}, f32[96,128]{1,0:T(8,128)S(1)}, u32[]{:S(2)}, u32[]{:S(2)}) collective-permute-start(f32[96,128]{1,0:T(8,128)S(1)} %get-tuple-element.8.r_3_), channel_id=1, source_target_pairs={{0,511},{32,0},{64,32},{96,64},{128,96},{160,128},{192,160},{224,1... | collective-permute-start | bytes 147464 | tf_op jit(solution)/shard_map/ppermute | solution.py:326
  66.4 0.1 maximum_maximum_fusion.1.r_1_
  66.5 0.0 collective-permute-done.1.r_2_
  66.5 1.1 collective-permute-done.2.r_5_
  67.6 16.9 %shard_map.80 = f32[384,128]{1,0:T(8,128)} custom-call(f32[64,64]{1,0:T(8,128)S(1)} %copy-done.5, f32[8,128]{1,0:T(8,128)S(1)} %maximum_maximum_fusion.1.r_1_, f32[96,128]{1,0:T(8,128)S(1)} %collective-permute-done.1.r_2_, f32[96,128]{1,0:T(8,128)S(1)} %get-tuple-element.8.r_3_, f32[96,128]{1,0:T(8,128)S(1)} %get-tuple-element.7.r_4_, ...), custom_call_target="tpu_custom_call" | custom-call | tf_op jit(solution)/shard_map/pallas_call | solution.py:338
  84.5 12.5 %all-to-all-start.1 = ((f32[32,3,4,128]{3,2,1,0:T(4,128)}), f32[32,3,4,128]{3,2,1,0:T(4,128)S(1)}, u32[]{:S(2)}, u32[]{:S(2)}) async-start(f32[32,3,4,128]{3,2,1,0:T(4,128)} %bitcast.8), calls=%async_computation.1 | async-start | bytes 393216 | tf_op jit(solution)/shard_map/all_to_all | solution.py:334
  97.1 0.0 copy-done
  97.1 0.1 pad.2.clone
  97.2 19.2 %all-to-all-done.1 = f32[32,3,4,128]{3,2,1,0:T(4,128)S(1)} async-done(((f32[32,3,4,128]{3,2,1,0:T(4,128)}), f32[32,3,4,128]{3,2,1,0:T(4,128)S(1)}, u32[]{:S(2)}, u32[]{:S(2)}) %all-to-all-start.1) | async-done | bytes 196640 | tf_op jit(solution)/shard_map/all_to_all | solution.py:334
  116.4 0.0 slice-start
  116.4 0.0 copy-start.1
  116.4 0.6 slice-done
  117.1 0.1 maximum_maximum_fusion
  117.1 2.3 %collective-permute-start.3 = (f32[16,128]{1,0:T(8,128)S(1)}, f32[16,128]{1,0:T(8,128)S(1)}, u32[]{:S(2)}, u32[]{:S(2)}) collective-permute-start(f32[16,128]{1,0:T(8,128)S(1)} %maximum_maximum_fusion), channel_id=1, source_target_pairs={{0,15},{1,0},{2,1},{3,2},{4,3},{5,4},{6,5},{7,6},{8,7},{9,8},{10,9... | collective-permute-start | bytes 24584 | tf_op jit(solution)/shard_map/ppermute | solution.py:330
  119.4 2.7 %collective-permute-done.3.r_1_ = f32[16,128]{1,0:T(8,128)S(1)} collective-permute-done((f32[16,128]{1,0:T(8,128)S(1)}, f32[16,128]{1,0:T(8,128)S(1)}, u32[]{:S(2)}, u32[]{:S(2)}) %collective-permute-start.3) | collective-permute-done | bytes 8224 | tf_op jit(solution)/shard_map/ppermute | solution.py:330
  122.1 0.0 copy-done.1
  122.1 14.5 %shard_map.81 = (f32[3,64,128]{2,1,0:T(8,128)}, f32[3,64,128]{2,1,0:T(8,128)}) custom-call(f32[384,128]{1,0:T(8,128)S(1)} %bitcast.16, f32[16,128]{1,0:T(8,128)S(1)} %collective-permute-done.3.r_1_, f32[16,128]{1,0:T(8,128)S(1)} %collective-permute-done.r_0_.r_2_, f32[64,128]{1,0:T(8,128)S(1)} %copy-done.1, f32[64,128]{1,0:T(8,128)S(1)} %divide_multiply_fusion.r_3_.r_4_), custom_call_target="tpu_custom_call" | custom-call | tf_op jit(solution)/shard_map/pallas_call | solution.py:338
  (10 shorter events, 0.1 us)
Async XLA Ops:
  0.6 0.8 copy-start.7
  0.6 0.8 copy-start.6
  0.7 0.9 copy-start.2
  1.4 95.6 %copy-start = (f32[64,128]{1,0:T(8,128)}, f32[64,128]{1,0:T(8,128)S(1)}, u32[]{:S(2)}) copy-start(f32[64,128]{1,0:T(8,128)S(1)} %fusion.r_2_.r_3_) | copy-start | bytes 98308
  1.6 0.9 copy-start.3
  2.5 9.6 %copy-start.4 = (f32[1,64,3,128]{3,1,2,0:T(8,128)S(1)}, f32[1,64,3,128]{3,1,2,0:T(8,128)}, u32[]{:S(2)}) copy-start(f32[1,64,3,128]{3,1,2,0:T(8,128)} %param.7) | copy-start | bytes 294916
  2.5 9.6 %collective-permute-start = (f32[16,128]{1,0:T(8,128)S(1)}, f32[16,128]{1,0:T(8,128)S(1)}, u32[]{:S(2)}, u32[]{:S(2)}) collective-permute-start(f32[16,128]{1,0:T(8,128)S(1)} %shard_map.77), channel_id=1, source_target_pairs={{0,1},{1,2},{2,3},{3,4},{4,5},{5,6},{6,7},{7,8},{8,9},{9,10},{10,1... | collective-permute-start | bytes 24584 | tf_op jit(solution)/shard_map/ppermute | solution.py:330
  26.5 29.1 %all-to-all-start = ((f32[32,3,4,128]{3,2,1,0:T(4,128)}), f32[32,3,4,128]{3,2,1,0:T(4,128)S(1)}, u32[]{:S(2)}, u32[]{:S(2)}) async-start(f32[32,3,4,128]{3,2,1,0:T(4,128)} %bitcast.6), calls=%async_computation | async-start | bytes 393216 | tf_op jit(solution)/shard_map/all_to_all | solution.py:334
  40.2 15.4 %copy-start.5 = (f32[64,64]{1,0:T(8,128)S(1)}, f32[64,64]{1,0:T(8,128)}, u32[]{:S(2)}) copy-start(f32[64,64]{1,0:T(8,128)} %constant.47.clone.r_0_) | copy-start | bytes 49156
  55.9 10.6 %collective-permute-start.1 = (f32[96,128]{1,0:T(8,128)S(1)}, f32[96,128]{1,0:T(8,128)S(1)}, u32[]{:S(2)}, u32[]{:S(2)}) collective-permute-start(f32[96,128]{1,0:T(8,128)S(1)} %get-tuple-element.7.r_4_), channel_id=1, source_target_pairs={{0,32},{32,64},{64,96},{96,128},{128,160},{160,192},{192,224},{224... | collective-permute-start | bytes 147464 | tf_op jit(solution)/shard_map/ppermute | solution.py:326
  58.0 9.6 %collective-permute-start.2 = (f32[96,128]{1,0:T(8,128)S(1)}, f32[96,128]{1,0:T(8,128)S(1)}, u32[]{:S(2)}, u32[]{:S(2)}) collective-permute-start(f32[96,128]{1,0:T(8,128)S(1)} %get-tuple-element.8.r_3_), channel_id=1, source_target_pairs={{0,511},{32,0},{64,32},{96,64},{128,96},{160,128},{192,160},{224,1... | collective-permute-start | bytes 147464 | tf_op jit(solution)/shard_map/ppermute | solution.py:326
  84.5 31.9 %all-to-all-start.1 = ((f32[32,3,4,128]{3,2,1,0:T(4,128)}), f32[32,3,4,128]{3,2,1,0:T(4,128)S(1)}, u32[]{:S(2)}, u32[]{:S(2)}) async-start(f32[32,3,4,128]{3,2,1,0:T(4,128)} %bitcast.8), calls=%async_computation.1 | async-start | bytes 393216 | tf_op jit(solution)/shard_map/all_to_all | solution.py:334
  116.4 0.7 slice-start
  116.4 5.7 %copy-start.1 = (f32[64,128]{1,0:T(8,128)S(1)}, f32[64,128]{1,0:T(8,128)}, u32[]{:S(2)}) copy-start(f32[64,128]{1,0:T(8,128)} %copy-done) | copy-start | bytes 98308
  117.1 5.0 %collective-permute-start.3 = (f32[16,128]{1,0:T(8,128)S(1)}, f32[16,128]{1,0:T(8,128)S(1)}, u32[]{:S(2)}, u32[]{:S(2)}) collective-permute-start(f32[16,128]{1,0:T(8,128)S(1)} %maximum_maximum_fusion), channel_id=1, source_target_pairs={{0,15},{1,0},{2,1},{3,2},{4,3},{5,4},{6,5},{7,6},{8,7},{9,8},{10,9... | collective-permute-start | bytes 24584 | tf_op jit(solution)/shard_map/ppermute | solution.py:330

commit v2 on v1

v2 whole, which is shorter than its diff:
```python
import math

import jax
import jax.numpy as jnp
import numpy as np
from jax import lax
from jax.experimental import pallas as pl
from jax.experimental.pallas import tpu as pltpu
from jax.sharding import PartitionSpec as P

STEPS = 2

time_step = 1.5
cycle_omega = 6.0
strength = 0.01
width_sq = 0.25

F32 = jnp.float32
BF16 = jnp.bfloat16
LANES = 128
ROWS = 24
SPAN = 12
WIDE = 24
ALPHA = math.sqrt(math.log2(math.e) / width_sq)
GAIN = strength / width_sq / ALPHA
FAR = 1e12


def cycle_matrix(count):
    j = np.arange(count, dtype=np.float64)[:, None]
    k = np.arange(count, dtype=np.float64)[None, :]
    half = count // 2
    phase = 2.0 * np.pi * j * k / count
    table = np.where(
        k < half, np.sqrt(2.0 / count) * np.cos(phase), np.sqrt(2.0 / count) * np.sin(phase)
    )
    table = np.where(k == 0, 1.0 / np.sqrt(count), table)
    table = np.where(k == half, np.cos(np.pi * j) / np.sqrt(count), table)
    omega = 2.0 * cycle_omega * np.sin(np.pi * k[0] / count)
    angle = omega * time_step
    to_position = np.where(k[0] == 0, time_step, np.sin(angle) / np.where(k[0] == 0, 1.0, omega))
    same = (table * np.cos(angle)) @ table.T
    from_velocity = (table * to_position) @ table.T
    from_position = (table * (-omega * np.sin(angle))) @ table.T
    return np.block([[same, from_velocity], [from_position, same]]).astype(np.float32)


def split3(value):
    high = value.astype(BF16).astype(F32)
    rest = value - high
    mid = rest.astype(BF16).astype(F32)
    low = (rest - mid).astype(BF16).astype(F32)
    return high, mid, low


def put_tables(planes, occupied, tables, start, stride=1):
    left, right, moved = tables
    count = planes[0].shape[0]
    one = jnp.ones_like(planes[0])

    def put(ref, row, value):
        ref[pl.ds(start * ROWS + row, count, stride=stride * ROWS), :] = value

    def norm(parts):
        total = parts[0] * parts[0] + parts[1] * parts[1] + parts[2] * parts[2]
        return split3(-0.5 * total - FAR * (1.0 - occupied))

    scaled = [ALPHA * plane for plane in planes]
    pieces = [split3(part) for part in scaled]
    norms = norm(scaled)
    for axis in range(3):
        high, mid, low = pieces[axis]
        for row, value in ((0, high), (4, mid), (8, high), (12, low), (16, high), (20, mid)):
            put(left, row + axis, value)
        for row, value in ((0, high), (4, high), (8, mid), (12, high), (16, low), (20, mid)):
            put(right, row + axis, value)
            if axis:
                put(moved, row + axis, value)
    for piece in range(3):
        put(left, 8 * piece + 3, norms[piece])
        put(left, 8 * piece + 7, one)
        put(right, 8 * piece + 3, one)
        put(right, 8 * piece + 7, norms[piece])
        put(moved, 8 * piece + 3, one)
    ahead = ALPHA * (planes[0] + 1.0)
    high, mid, low = split3(ahead)
    for row, value in ((0, high), (4, high), (8, mid), (12, high), (16, low), (20, mid)):
        put(moved, row, value)
    norms = norm([ahead, scaled[1], scaled[2]])
    for piece in range(3):
        put(moved, 8 * piece + 7, norms[piece])


def table_rows(ref, cell):
    return ref[cell * ROWS : (cell + 1) * ROWS, :]


def factor(table):
    pad = jnp.zeros((8, LANES), F32)
    return jnp.concatenate([table, pad], axis=0).astype(BF16)


def put_weights(tables, weights, index, own, near, full):
    left, right, moved = tables
    others = factor(table_rows(moved, near))
    if full:
        others = jnp.concatenate([factor(table_rows(right, own)), others], axis=1)
    exponent = lax.dot_general(
        factor(table_rows(left, own)),
        others,
        (((0,), (0,)), ((), ())),
        preferred_element_type=F32,
    )
    start = 0 if full else LANES
    weights[index * LANES : (index + 1) * LANES, start:] = jnp.exp2(exponent).astype(BF16)


def fold(sums):
    return sums[0:8], sums[0:8] + sums[8:16] + sums[16:24]


def own_sums(tables, weights, index, own, near):
    both = jnp.concatenate(
        [factor(table_rows(tables[1], own)), factor(table_rows(tables[2], near))], axis=1
    )
    weight = weights[index * LANES : (index + 1) * LANES, :]
    return fold(
        lax.dot_general(both, weight, (((1,), (1,)), ((), ())), preferred_element_type=F32)
    )


def next_sums(tables, weights, index, own):
    weight = weights[index * LANES : (index + 1) * LANES, LANES:]
    return fold(
        lax.dot_general(
            factor(table_rows(tables[1], own)),
            weight,
            (((1,), (0,)), ((), ())),
            preferred_element_type=F32,
        )
    )


def force_of(tables, own, sums, carry):
    table = table_rows(tables[1], own)
    place = table[0:8] + table[8:16] + table[16:24]
    shift = jnp.where(lax.broadcasted_iota(jnp.int32, (8, LANES), 0) == 0, ALPHA, 0.0)
    from_right = place * sums[0][3:4] - sums[1]
    from_left = (place + shift) * carry[0][3:4] - carry[1]
    return GAIN * (from_right + from_left)


def chain_forces(tables, weights, chains, emit, group):
    steps = [
        (own, own > first, own + 1 < last)
        for first, last in chains
        for own in range(first, last)
    ]
    carry = None
    for start in range(0, len(steps), group):
        part = list(enumerate(steps))[start : start + group]
        for index, (own, inner, _) in part:
            put_weights(tables, weights, index, own, own + 1, inner)
        for index, (own, inner, more) in part:
            if inner:
                sums = own_sums(tables, weights, index, own, own + 1)
                emit(own, force_of(tables, own, sums, carry))
            carry = next_sums(tables, weights, index, own) if more else None


def scratch(rows):
    return pltpu.VMEM((rows, LANES), F32)


VMEM = pl.BlockSpec(memory_space=pltpu.VMEM)
PARAMS = pltpu.CompilerParams(vmem_limit_bytes=48 * 1024 * 1024)


def edge_kernel(cells, pos_ref, vel_ref, occ_ref, kick_ref, out_ref):
    for axis in range(3):
        out_ref[axis * 4 : axis * 4 + 4, :] = pos_ref[axis, cells - 4 : cells, :]
        out_ref[12 + axis * 3 : 15 + axis * 3, :] = vel_ref[axis, cells - 3 : cells, :]
    out_ref[21:24, :] = kick_ref[cells - 3 : cells, :]
    out_ref[24:28, :] = occ_ref[cells - 4 : cells, :]
    out_ref[28:32, :] = jnp.zeros((4, LANES), F32)


def first_kernel(
    cells, edge_ref, pos_ref, vel_ref, occ_ref, kick_ref, send_ref,
    place, speed, occ_all, weights, left, right, moved,
):
    half = cells // 4
    for axis in range(3):
        place[pl.ds(axis, 4, stride=8), :] = edge_ref[axis * 4 : axis * 4 + 4, :]
        place[pl.ds(4 * 8 + axis, cells, stride=8), :] = pos_ref[axis]
        speed[pl.ds(8 + axis, 3, stride=8), :] = edge_ref[12 + axis * 3 : 15 + axis * 3, :]
        speed[pl.ds(4 * 8 + axis, cells, stride=8), :] = vel_ref[axis]
    place[pl.ds(8 + 3, 3, stride=8), :] = edge_ref[21:24, :]
    place[pl.ds(4 * 8 + 3, cells, stride=8), :] = kick_ref[...]
    occ_all[0:4, :] = edge_ref[24:28, :]
    occ_all[4 : cells + 4, :] = occ_ref[...]
    tables = (left, right, moved)
    count = cells + 8
    planes = [place[pl.ds(axis, count, stride=8), :] for axis in range(3)]
    put_tables(planes, occ_all[...], tables, 0)

    def emit(slot, force):
        rows = slice(slot * 8, slot * 8 + 8)
        speed[rows, :] = speed[rows, :] + place[rows, :][3:4] * force

    chain_forces(tables, weights, [(0, cells + 3)], emit, 13)
    for kind, source in enumerate((place, speed)):
        for axis in range(3):
            for near in range(4):
                row = (kind * 3 + axis) * 4 + near
                for part in range(2):
                    first = (part * 2 * half + 1 + near) * 8 + axis
                    send_ref[pl.ds(part * WIDE + row, half, stride=2 * WIDE), :] = source[
                        pl.ds(first, half, stride=16), :
                    ]


def cycle(matrix, blocks):
    return jnp.dot(
        matrix,
        jnp.concatenate(blocks, axis=1),
        precision=lax.Precision.HIGHEST,
        preferred_element_type=F32,
    )


def lanes_of(array, index):
    return array[:, index * LANES : (index + 1) * LANES]


def middle_kernel(
    images, matrix_ref, info_ref, got_ref, send_ref, forces, weights, left, right, moved
):
    tables = (left, right, moved)

    def blocks_of(slots):
        return [
            jnp.concatenate(
                [
                    got_ref[pl.ds((kind * 3 + axis) * 4 + slot, images, stride=WIDE), :]
                    for kind in range(2)
                ],
                axis=0,
            )
            for slot in slots
            for axis in range(3)
        ]

    inner = cycle(matrix_ref[...], blocks_of((1, 2)))
    outer = cycle(matrix_ref[:images, :], blocks_of((0, 3)))
    for slot in range(4):
        source, first = ((outer, 0), (inner, 0), (inner, 3), (outer, 3))[slot]
        planes = [lanes_of(source, first + axis)[:images] for axis in range(3)]
        occupied = jnp.broadcast_to(info_ref[slot : slot + 1, :], (images, LANES))
        put_tables(planes, occupied, tables, slot, stride=4)

    def emit(cell, force):
        row = (cell // 4 * 2 + cell % 4 - 1) * 8
        forces[row : row + 8, :] = force

    chains = [(4 * image, 4 * image + 3) for image in range(images)]
    chain_forces(tables, weights, chains, emit, 12)
    blocks = []
    for parity in range(2):
        kick = 2.0 * info_ref[4 + parity : 5 + parity, :]
        for axis in range(3):
            now = lanes_of(inner, parity * 3 + axis)
            force = forces[pl.ds(parity * 8 + axis, images, stride=16), :]
            blocks.append(jnp.concatenate([now[:images], now[images:] + kick * force], axis=0))
    ahead = cycle(matrix_ref[...], blocks)
    for parity in range(2):
        for axis in range(3):
            after = lanes_of(ahead, parity * 3 + axis)
            for kind in range(2):
                row = (kind * 3 + axis) * 2 + parity
                send_ref[pl.ds(row, images, stride=SPAN), :] = after[
                    kind * images : (kind + 1) * images
                ]


def last_kernel(
    cells, got_ref, edge_ref, first_ref, occ_ref, kick_ref, pos_ref, vel_ref,
    place, speed, occ_all, weights, left, right, moved,
):
    half = cells // 4
    for kind, target in enumerate((place, speed)):
        for axis in range(3):
            for parity in range(2):
                row = (kind * 3 + axis) * 2 + parity
                for part in range(2):
                    first = (part * 2 * half + parity) * 8 + axis
                    target[pl.ds(first, half, stride=16), :] = got_ref[
                        pl.ds(part * SPAN + row, half, stride=2 * SPAN), :
                    ]
                slot = (cells + parity) * 8 + axis
                target[slot : slot + 1, :] = edge_ref[row : row + 1, :]
    for axis in range(3):
        slot = (cells + 2) * 8 + axis
        place[slot : slot + 1, :] = edge_ref[12 + axis : 13 + axis, :]
    place[pl.ds(2 * 8 + 3, cells, stride=8), :] = kick_ref[...]
    occ_all[0:2, :] = first_ref[26:28, :]
    occ_all[2 : cells + 2, :] = occ_ref[...]
    occ_all[cells + 2 : cells + 3, :] = edge_ref[15:16, :]
    tables = (left, right, moved)
    count = cells + 8
    planes = [place[pl.ds(axis, count, stride=8), :] for axis in range(3)]
    put_tables(planes, occ_all[...], tables, 0)

    def emit(slot, force):
        rows = slice(slot * 8, slot * 8 + 8)
        speed[rows, :] = speed[rows, :] + place[rows, :][3:4] * force

    chain_forces(tables, weights, [(1, cells + 2)], emit, 13)
    for axis in range(3):
        pos_ref[axis] = place[pl.ds(2 * 8 + axis, cells, stride=8), :]
        vel_ref[axis] = speed[pl.ds(2 * 8 + axis, cells, stride=8), :]


def local(positions, velocities, counts, types, masses):
    images = lax.axis_size("image")
    slabs = lax.axis_size("space")
    cells = positions.shape[1]
    rows = cells + 8

    def slab_shift(array, distance):
        pairs = [(s, (s + distance) % slabs) for s in range(slabs)]
        return lax.ppermute(array, "space", pairs)

    def transpose(array):
        blocks = array.reshape(images, array.shape[0] // images // 4, 4, LANES)
        blocks = lax.all_to_all(blocks, "image", split_axis=0, concat_axis=0, tiled=True)
        return blocks.reshape(array.shape)

    def call(kernel, outs, scratches, *args):
        return pl.pallas_call(
            kernel,
            out_shape=outs,
            in_specs=[VMEM] * len(args),
            out_specs=jax.tree.map(lambda _: VMEM, outs),
            scratch_shapes=scratches,
            compiler_params=PARAMS,
        )(*args)

    def shaped(*shape):
        return jax.ShapeDtypeStruct(shape, F32)

    def weight_scratch(steps):
        return pltpu.VMEM((steps * LANES, 2 * LANES), BF16)

    slot_index = lax.broadcasted_iota(jnp.int32, types.shape, 1)
    occupied = (slot_index < counts[:, None]).astype(F32)
    type_index = lax.broadcasted_iota(jnp.int32, (masses.shape[0],) + types.shape, 0)
    chosen = jnp.sum(jnp.where(types[None] == type_index, masses[:, None, None], 0.0), axis=0)
    kick = 0.5 * time_step * (1.0 / chosen)
    matrix = jnp.asarray(cycle_matrix(images))
    group = lax.axis_index("image")
    block = (group % 2) * (images // 2) + group // 2

    pos = positions[0].transpose(1, 0, 2)
    vel = velocities[0].transpose(1, 0, 2)
    slab_scratch = [scratch(rows * 8), scratch(rows * 8), scratch(rows), weight_scratch(rows)]
    slab_scratch += [scratch(rows * ROWS)] * 3
    edge = call(lambda *r: edge_kernel(cells, *r), shaped(32, LANES), [], pos, vel, occupied, kick)
    edge = slab_shift(edge, 1)
    send = call(
        lambda *r: first_kernel(cells, *r),
        shaped(images * WIDE, LANES),
        slab_scratch,
        edge, pos, vel, occupied, kick,
    )
    got = transpose(send)
    occ_wide = jnp.concatenate([edge[24:28], occupied], axis=0)
    kick_wide = jnp.concatenate([edge[21:24], kick], axis=0)
    info = jnp.concatenate(
        [
            lax.dynamic_slice_in_dim(occ_wide, 2 * block + 1, 4, 0),
            lax.dynamic_slice_in_dim(kick_wide, 2 * block + 1, 2, 0),
            jnp.zeros((2, LANES), F32),
        ],
        axis=0,
    )
    send = call(
        lambda *r: middle_kernel(images, *r),
        shaped(images * SPAN, LANES),
        [scratch(2 * images * 8), weight_scratch(3 * images)] + [scratch(4 * images * ROWS)] * 3,
        matrix, info, got,
    )
    got = transpose(send)
    chunk = 2 * SPAN
    message = jnp.concatenate(
        [got[0:SPAN]]
        + [got[chunk + 2 * axis : chunk + 2 * axis + 1] for axis in range(3)]
        + [occupied[0:1]],
        axis=0,
    )
    message = slab_shift(message, -1)
    pos, vel = call(
        lambda *r: last_kernel(cells, *r),
        (shaped(*pos.shape), shaped(*vel.shape)),
        slab_scratch,
        got, message, edge, occupied, kick,
    )
    return pos.transpose(1, 0, 2)[None], vel.transpose(1, 0, 2)[None]


def solution(mesh):
    return jax.shard_map(
        local,
        mesh=mesh,
        in_specs=(
            P("image", "space", None, None),
            P("image", "space", None, None),
            P("space"),
            P("space", None),
            P(),
        ),
        out_specs=(P("image", "space", None, None), P("image", "space", None, None)),
        check_vma=False,
    )
```

time: 137 us -> 99.7 us (0.73)
  Pallas kernels: 46.2 us -> 16.3 us
  starting transfers between devices: 43.6 us -> 33 us
  waiting for transfers between devices: 43.1 us -> 45.8 us
    pallas_call x5 -> x4, Pallas kernels: 46.2 us -> 16.3 us  [call(): pl.pallas_call(kernel, out_shape=outs, in_specs=[VMEM] * len(args), out_s...]
    ppermute x2 -> x0, starting transfers between devices: 10.5 us -> none  [shift(): return lax.ppermute(array, ('image', 'space'), pairs)]
    all_to_all x2, starting transfers between devices: 26.1 us -> 21 us  [transpose(): lax.all_to_all(blocks, 'image', split_axis=0, concat_axis=0, tiled=True)]
    ppermute x2, starting transfers between devices: 7.02 us -> 12 us  [slab_shift(): return lax.ppermute(array, 'space', pairs)]
    all_to_all x2, waiting for transfers between devices: 34.6 us -> 37.7 us  [transpose(): lax.all_to_all(blocks, 'image', split_axis=0, concat_axis=0, tiled=True)]
  transfers between devices with their start and end apart: 6 -> 4, of which waited for: 5 -> 4; matrix products, arithmetic and copies ran while one was open for 0% -> 0% of each run, Pallas kernels for 0% -> 0%
where the time goes in v2:
time: 99.7 us; the launch traced here: 99.2 us
  waiting for transfers between devices  45.8 us (46%)
  starting transfers between devices  33 us (33%)
  Pallas kernels  16.3 us (16%)
  local copies, waits for them, and re-layouts  2.35 us (2%)
    all_to_all x2, waiting for transfers between devices, transpose(): lax.all_to_all(blocks, 'image', split_axis=0, concat_axis=0, tiled=True)  37.7 us
    all_to_all x2, starting transfers between devices, transpose(): lax.all_to_all(blocks, 'image', split_axis=0, concat_axis=0, tiled=True)  21 us
    pallas_call x4, Pallas kernels, call(): pl.pallas_call(kernel, out_shape=outs, in_specs=[VMEM] * len(args), out_s...  16.3 us
    ppermute x2, starting transfers between devices, slab_shift(): return lax.ppermute(array, 'space', pairs)  12 us
    ppermute x2, waiting for transfers between devices, slab_shift(): return lax.ppermute(array, 'space', pairs)  8.13 us
  transfers between devices with their start and end apart: 4, of which 4 were waited for; matrix products, arithmetic and copies ran while one was open for 0% of the time, Pallas kernels for 0%

profile of v2, /device:TPU:1, one launch (start us, length us, event | category | flops | bytes accessed | tf_op | source)
XLA Modules:
  0.0 99.2 jit_solution(7186287473075281319)
XLA Ops:
  0.6 0.0 copy-start.8
  0.6 0.0 copy-start.7
  0.7 0.0 copy-start.2
  0.7 0.8 fusion.r_2_.r_3_
  1.4 0.0 copy-done.8
  1.4 0.0 copy-done.7
  1.4 0.0 copy-start
  1.5 0.1 select_reduce_fusion
  1.6 0.0 copy-done.2
  1.6 0.0 copy-start.3
  1.6 0.9 copy-done.3
  2.5 4.6 %collective-permute-start = (f32[32,128]{1,0:T(8,128)S(1)}, f32[32,128]{1,0:T(8,128)S(1)}, u32[]{:S(2)}, u32[]{:S(2)}) collective-permute-start(f32[32,128]{1,0:T(8,128)S(1)} %shard_map.77), channel_id=1, source_target_pairs={{0,1},{1,2},{2,3},{3,4},{4,5},{5,6},{6,7},{7,8},{8,9},{9,10},{10,1... | collective-permute-start | bytes 49160 | tf_op jit(solution)/shard_map/ppermute | solution.py:332
  7.1 4.9 %collective-permute-done.r_0_.r_2_ = f32[32,128]{1,0:T(8,128)S(1)} collective-permute-done((f32[32,128]{1,0:T(8,128)S(1)}, f32[32,128]{1,0:T(8,128)S(1)}, u32[]{:S(2)}, u32[]{:S(2)}) %collective-permute-start) | collective-permute-done | bytes 16416 | tf_op jit(solution)/shard_map/ppermute | solution.py:332
  11.9 0.0 copy-start.4
  11.9 4.4 %shard_map.78 = f32[768,128]{1,0:T(8,128)} custom-call(f32[32,128]{1,0:T(8,128)S(1)} %collective-permute-done.r_0_.r_2_, f32[3,64,128]{2,1,0:T(8,128)S(1)} %bitcast.20, f32[3,64,128]{2,1,0:T(8,128)S(1)} %bitcast.22, f32[64,128]{1,0:T(8,128)S(1)} %fusion.r_2_.r_3_, f32[64,128]{1,0:T(8,128)S(1)} %divide_multiply_fusion.r_3_.r_4_), custom_call_target="tpu_custom_call" | custom-call | tf_op jit(solution)/shard_map/pallas_call | solution.py:340
  16.4 13.6 %all-to-all-start = ((f32[32,6,4,128]{3,2,1,0:T(4,128)}), f32[32,6,4,128]{3,2,1,0:T(4,128)S(1)}, u32[]{:S(2)}, u32[]{:S(2)}) async-start(f32[32,6,4,128]{3,2,1,0:T(4,128)} %bitcast.6), calls=%async_computation | async-start | bytes 786432 | tf_op jit(solution)/shard_map/all_to_all | solution.py:336
  30.1 0.1 pad.2.clone
  30.1 0.0 copy-done.4
  30.1 0.0 slice-start.1
  30.1 0.0 copy-start.6
  30.2 0.6 slice-done.1
  30.8 0.1 maximum_maximum_fusion.r_1_
  30.9 22.2 %all-to-all-done = f32[32,6,4,128]{3,2,1,0:T(4,128)S(1)} async-done(((f32[32,6,4,128]{3,2,1,0:T(4,128)}), f32[32,6,4,128]{3,2,1,0:T(4,128)S(1)}, u32[]{:S(2)}, u32[]{:S(2)}) %all-to-all-start) | async-done | bytes 393248 | tf_op jit(solution)/shard_map/all_to_all | solution.py:336
  53.1 0.0 copy-done.6
  53.1 7.7 %shard_map.79 = f32[384,128]{1,0:T(8,128)} custom-call(f32[64,64]{1,0:T(8,128)S(1)} %copy-done.6, f32[8,128]{1,0:T(8,128)S(1)} %maximum_maximum_fusion.r_1_, f32[768,128]{1,0:T(8,128)S(1)} %bitcast.16), custom_call_target="tpu_custom_call" | custom-call | tf_op jit(solution)/shard_map/pallas_call | solution.py:340
  60.8 7.3 %all-to-all-start.1 = ((f32[32,3,4,128]{3,2,1,0:T(4,128)}), f32[32,3,4,128]{3,2,1,0:T(4,128)S(1)}, u32[]{:S(2)}, u32[]{:S(2)}) async-start(f32[32,3,4,128]{3,2,1,0:T(4,128)} %bitcast.8), calls=%async_computation.1 | async-start | bytes 393216 | tf_op jit(solution)/shard_map/all_to_all | solution.py:336
  68.1 0.0 copy-done
  68.1 0.0 copy-start.1
  68.2 15.5 %all-to-all-done.1 = f32[32,3,4,128]{3,2,1,0:T(4,128)S(1)} async-done(((f32[32,3,4,128]{3,2,1,0:T(4,128)}), f32[32,3,4,128]{3,2,1,0:T(4,128)S(1)}, u32[]{:S(2)}, u32[]{:S(2)}) %all-to-all-start.1) | async-done | bytes 196640 | tf_op jit(solution)/shard_map/all_to_all | solution.py:336
  83.6 0.0 slice-start
  83.7 0.0 copy-start.5
  83.7 0.6 slice-done
  84.3 7.4 %collective-permute-start.1 = (f32[16,128]{1,0:T(8,128)S(1)}, f32[16,128]{1,0:T(8,128)S(1)}, u32[]{:S(2)}, u32[]{:S(2)}) collective-permute-start(f32[16,128]{1,0:T(8,128)S(1)} %concatenate.15), channel_id=1, source_target_pairs={{0,15},{1,0},{2,1},{3,2},{4,3},{5,4},{6,5},{7,6},{8,7},{9,8},{10,9... | collective-permute-start | bytes 24584 | tf_op jit(solution)/shard_map/ppermute | solution.py:332
  91.8 3.3 %collective-permute-done.1.r_1_ = f32[16,128]{1,0:T(8,128)S(1)} collective-permute-done((f32[16,128]{1,0:T(8,128)S(1)}, f32[16,128]{1,0:T(8,128)S(1)}, u32[]{:S(2)}, u32[]{:S(2)}) %collective-permute-start.1) | collective-permute-done | bytes 8224 | tf_op jit(solution)/shard_map/ppermute | solution.py:332
  95.0 0.0 copy-done.1
  95.0 0.0 copy-done.5
  95.0 4.2 %shard_map.80 = (f32[3,64,128]{2,1,0:T(8,128)}, f32[3,64,128]{2,1,0:T(8,128)}) custom-call(f32[384,128]{1,0:T(8,128)S(1)} %bitcast.18, f32[16,128]{1,0:T(8,128)S(1)} %collective-permute-done.1.r_1_, f32[32,128]{1,0:T(8,128)S(1)} %copy-done.5, f32[64,128]{1,0:T(8,128)S(1)} %copy-done.1, f32[64,128]{1,0:T(8,128)S(1)} %divide_multiply_fusion.r_3_.r_4_), custom_call_target="tpu_custom_call" | custom-call | tf_op jit(solution)/shard_map/pallas_call | solution.py:340
  (10 shorter events, 0.1 us)
Async XLA Ops:
  0.6 0.8 copy-start.8
  0.6 0.8 copy-start.7
  0.7 0.9 copy-start.2
  1.4 66.7 %copy-start = (f32[64,128]{1,0:T(8,128)}, f32[64,128]{1,0:T(8,128)S(1)}, u32[]{:S(2)}) copy-start(f32[64,128]{1,0:T(8,128)S(1)} %fusion.r_2_.r_3_) | copy-start | bytes 98308
  1.6 0.9 copy-start.3
  2.5 9.4 %collective-permute-start = (f32[32,128]{1,0:T(8,128)S(1)}, f32[32,128]{1,0:T(8,128)S(1)}, u32[]{:S(2)}, u32[]{:S(2)}) collective-permute-start(f32[32,128]{1,0:T(8,128)S(1)} %shard_map.77), channel_id=1, source_target_pairs={{0,1},{1,2},{2,3},{3,4},{4,5},{5,6},{6,7},{7,8},{8,9},{9,10},{10,1... | collective-permute-start | bytes 49160 | tf_op jit(solution)/shard_map/ppermute | solution.py:332
  11.9 18.2 %copy-start.4 = (f32[32,128]{1,0:T(8,128)}, f32[32,128]{1,0:T(8,128)S(1)}, u32[]{:S(2)}) copy-start(f32[32,128]{1,0:T(8,128)S(1)} %collective-permute-done.r_0_.r_2_) | copy-start | bytes 49156
  16.4 36.7 %all-to-all-start = ((f32[32,6,4,128]{3,2,1,0:T(4,128)}), f32[32,6,4,128]{3,2,1,0:T(4,128)S(1)}, u32[]{:S(2)}, u32[]{:S(2)}) async-start(f32[32,6,4,128]{3,2,1,0:T(4,128)} %bitcast.6), calls=%async_computation | async-start | bytes 786432 | tf_op jit(solution)/shard_map/all_to_all | solution.py:336
  30.1 0.7 slice-start.1
  30.1 23.0 %copy-start.6 = (f32[64,64]{1,0:T(8,128)S(1)}, f32[64,64]{1,0:T(8,128)}, u32[]{:S(2)}) copy-start(f32[64,64]{1,0:T(8,128)} %constant.49.clone.r_0_) | copy-start | bytes 49156
  60.8 22.8 %all-to-all-start.1 = ((f32[32,3,4,128]{3,2,1,0:T(4,128)}), f32[32,3,4,128]{3,2,1,0:T(4,128)S(1)}, u32[]{:S(2)}, u32[]{:S(2)}) async-start(f32[32,3,4,128]{3,2,1,0:T(4,128)} %bitcast.8), calls=%async_computation.1 | async-start | bytes 393216 | tf_op jit(solution)/shard_map/all_to_all | solution.py:336
  68.1 26.9 %copy-start.1 = (f32[64,128]{1,0:T(8,128)S(1)}, f32[64,128]{1,0:T(8,128)}, u32[]{:S(2)}) copy-start(f32[64,128]{1,0:T(8,128)} %copy-done) | copy-start | bytes 98308
  83.6 0.7 slice-start
  83.7 11.4 %copy-start.5 = (f32[32,128]{1,0:T(8,128)S(1)}, f32[32,128]{1,0:T(8,128)}, u32[]{:S(2)}) copy-start(f32[32,128]{1,0:T(8,128)} %copy-done.4) | copy-start | bytes 49156
  84.3 10.7 %collective-permute-start.1 = (f32[16,128]{1,0:T(8,128)S(1)}, f32[16,128]{1,0:T(8,128)S(1)}, u32[]{:S(2)}, u32[]{:S(2)}) collective-permute-start(f32[16,128]{1,0:T(8,128)S(1)} %concatenate.15), channel_id=1, source_target_pairs={{0,15},{1,0},{2,1},{3,2},{4,3},{5,4},{6,5},{7,6},{8,7},{9,8},{10,9... | collective-permute-start | bytes 24584 | tf_op jit(solution)/shard_map/ppermute | solution.py:332

commit v3 on v2

--- a/solution.py
+++ b/solution.py
@@ -20,6 +20,7 @@
 LANES = 128
 ROWS = 24
 SPAN = 12
+GROUP = 13
 WIDE = 24
 ALPHA = math.sqrt(math.log2(math.e) / width_sq)
 GAIN = strength / width_sq / ALPHA
@@ -144,18 +145,16 @@
 def force_of(tables, own, sums, carry):
     table = table_rows(tables[1], own)
     place = table[0:8] + table[8:16] + table[16:24]
-    shift = jnp.where(lax.broadcasted_iota(jnp.int32, (8, LANES), 0) == 0, ALPHA, 0.0)
-    from_right = place * sums[0][3:4] - sums[1]
-    from_left = (place + shift) * carry[0][3:4] - carry[1]
-    return GAIN * (from_right + from_left)
-
-
-def chain_forces(tables, weights, chains, emit, group):
-    steps = [
-        (own, own > first, own + 1 < last)
-        for first, last in chains
-        for own in range(first, last)
-    ]
+    total = 0.0
+    if sums is not None:
+        total = place * sums[0][3:4] - sums[1]
+    if carry is not None:
+        shift = jnp.where(lax.broadcasted_iota(jnp.int32, (8, LANES), 0) == 0, ALPHA, 0.0)
+        total = total + ((place + shift) * carry[0][3:4] - carry[1])
+    return GAIN * total
+
+
+def chain_forces(tables, weights, steps, emit, group):
     carry = None
     for start in range(0, len(steps), group):
         part = list(enumerate(steps))[start : start + group]
@@ -166,6 +165,7 @@
                 sums = own_sums(tables, weights, index, own, own + 1)
                 emit(own, force_of(tables, own, sums, carry))
             carry = next_sums(tables, weights, index, own) if more else None
+    return carry
 
 
 def scratch(rows):
@@ -176,39 +176,66 @@
 PARAMS = pltpu.CompilerParams(vmem_limit_bytes=48 * 1024 * 1024)
 
 
-def edge_kernel(cells, pos_ref, vel_ref, occ_ref, kick_ref, out_ref):
+def kick_of(types, mass_ref):
+    mass = jnp.zeros(types.shape, F32)
+    for kind in range(mass_ref.shape[0]):
+        mass = mass + jnp.where(types == kind, mass_ref[kind], 0.0)
+    return 0.5 * time_step / mass
+
+
+def edge_kernel(cells, count_ref, mass_ref, pos_ref, vel_ref, type_ref, out_ref):
     for axis in range(3):
-        out_ref[axis * 4 : axis * 4 + 4, :] = pos_ref[axis, cells - 4 : cells, :]
-        out_ref[12 + axis * 3 : 15 + axis * 3, :] = vel_ref[axis, cells - 3 : cells, :]
-    out_ref[21:24, :] = kick_ref[cells - 3 : cells, :]
-    out_ref[24:28, :] = occ_ref[cells - 4 : cells, :]
+        out_ref[axis * 4 : axis * 4 + 4, :] = pos_ref[axis, 4:8, :]
+        out_ref[12 + axis * 3 : 15 + axis * 3, :] = vel_ref[axis, 5:8, :]
+    out_ref[21:24, :] = kick_of(type_ref[...], mass_ref)[5:8]
+    slot = lax.broadcasted_iota(jnp.int32, (1, LANES), 1)
+    for near in range(4):
+        occupied = (slot < count_ref[cells - 4 + near]).astype(F32)
+        out_ref[24 + near : 25 + near, :] = occupied
     out_ref[28:32, :] = jnp.zeros((4, LANES), F32)
 
 
-def first_kernel(
-    cells, edge_ref, pos_ref, vel_ref, occ_ref, kick_ref, send_ref,
-    place, speed, occ_all, weights, left, right, moved,
-):
-    half = cells // 4
-    for axis in range(3):
-        place[pl.ds(axis, 4, stride=8), :] = edge_ref[axis * 4 : axis * 4 + 4, :]
-        place[pl.ds(4 * 8 + axis, cells, stride=8), :] = pos_ref[axis]
-        speed[pl.ds(8 + axis, 3, stride=8), :] = edge_ref[12 + axis * 3 : 15 + axis * 3, :]
-        speed[pl.ds(4 * 8 + axis, cells, stride=8), :] = vel_ref[axis]
-    place[pl.ds(8 + 3, 3, stride=8), :] = edge_ref[21:24, :]
-    place[pl.ds(4 * 8 + 3, cells, stride=8), :] = kick_ref[...]
-    occ_all[0:4, :] = edge_ref[24:28, :]
-    occ_all[4 : cells + 4, :] = occ_ref[...]
-    tables = (left, right, moved)
-    count = cells + 8
-    planes = [place[pl.ds(axis, count, stride=8), :] for axis in range(3)]
-    put_tables(planes, occ_all[...], tables, 0)
-
+def add_kick(place, speed):
     def emit(slot, force):
         rows = slice(slot * 8, slot * 8 + 8)
         speed[rows, :] = speed[rows, :] + place[rows, :][3:4] * force
 
-    chain_forces(tables, weights, [(0, cells + 3)], emit, 13)
+    return emit
+
+
+def first_inner_kernel(
+    cells, pos_ref, vel_ref, occ_ref, kick_ref, place, speed, weights, left, right, moved
+):
+    for axis in range(3):
+        place[pl.ds(4 * 8 + axis, cells, stride=8), :] = pos_ref[axis]
+        speed[pl.ds(4 * 8 + axis, cells, stride=8), :] = vel_ref[axis]
+    place[pl.ds(4 * 8 + 3, cells, stride=8), :] = kick_ref[...]
+    tables = (left, right, moved)
+    put_tables([pos_ref[axis] for axis in range(3)], occ_ref[...], tables, 4)
+    steps = [(own, True, own < cells + 2) for own in range(4, cells + 3)]
+    chain_forces(tables, weights, steps, add_kick(place, speed), GROUP)
+
+
+def first_outer_kernel(
+    cells, edge_ref, occ_ref, place_ref, speed_ref, send_ref,
+    place, speed, weights, left, right, moved,
+):
+    half = cells // 4
+    place[32:, :] = place_ref[32:, :]
+    speed[32:, :] = speed_ref[32:, :]
+    for axis in range(3):
+        place[pl.ds(axis, 4, stride=8), :] = edge_ref[axis * 4 : axis * 4 + 4, :]
+        speed[pl.ds(8 + axis, 3, stride=8), :] = edge_ref[12 + axis * 3 : 15 + axis * 3, :]
+    place[pl.ds(8 + 3, 3, stride=8), :] = edge_ref[21:24, :]
+    tables = (left, right, moved)
+    planes = [place[pl.ds(axis, 8, stride=8), :] for axis in range(3)]
+    occupied = jnp.concatenate([edge_ref[24:28, :], occ_ref[0:4, :]], axis=0)
+    put_tables(planes, occupied, tables, 0)
+    emit = add_kick(place, speed)
+    carry = chain_forces(
+        tables, weights, [(own, own > 0, True) for own in range(4)], emit, GROUP
+    )
+    emit(4, force_of(tables, 4, None, carry))
     for kind, source in enumerate((place, speed)):
         for axis in range(3):
             for near in range(4):
@@ -263,8 +290,10 @@
         row = (cell // 4 * 2 + cell % 4 - 1) * 8
         forces[row : row + 8, :] = force
 
-    chains = [(4 * image, 4 * image + 3) for image in range(images)]
-    chain_forces(tables, weights, chains, emit, 12)
+    steps = [
+        (4 * image + slot, slot > 0, slot < 2) for image in range(images) for slot in range(3)
+    ]
+    chain_forces(tables, weights, steps, emit, GROUP)
     blocks = []
     for parity in range(2):
         kick = 2.0 * info_ref[4 + parity : 5 + parity, :]
@@ -283,9 +312,9 @@
                 ]
 
 
-def last_kernel(
-    cells, got_ref, edge_ref, first_ref, occ_ref, kick_ref, pos_ref, vel_ref,
-    place, speed, occ_all, weights, left, right, moved,
+def last_inner_kernel(
+    cells, got_ref, first_ref, occ_ref, kick_ref, place, speed,
+    occ_all, weights, left, right, moved,
 ):
     half = cells // 4
     for kind, target in enumerate((place, speed)):
@@ -297,28 +326,56 @@
                     target[pl.ds(first, half, stride=16), :] = got_ref[
                         pl.ds(part * SPAN + row, half, stride=2 * SPAN), :
                     ]
-                slot = (cells + parity) * 8 + axis
-                target[slot : slot + 1, :] = edge_ref[row : row + 1, :]
-    for axis in range(3):
-        slot = (cells + 2) * 8 + axis
-        place[slot : slot + 1, :] = edge_ref[12 + axis : 13 + axis, :]
     place[pl.ds(2 * 8 + 3, cells, stride=8), :] = kick_ref[...]
     occ_all[0:2, :] = first_ref[26:28, :]
-    occ_all[2 : cells + 2, :] = occ_ref[...]
-    occ_all[cells + 2 : cells + 3, :] = edge_ref[15:16, :]
+    occ_all[2:cells, :] = occ_ref[: cells - 2, :]
     tables = (left, right, moved)
-    count = cells + 8
-    planes = [place[pl.ds(axis, count, stride=8), :] for axis in range(3)]
+    planes = [place[pl.ds(axis, cells, stride=8), :] for axis in range(3)]
     put_tables(planes, occ_all[...], tables, 0)
-
-    def emit(slot, force):
-        rows = slice(slot * 8, slot * 8 + 8)
-        speed[rows, :] = speed[rows, :] + place[rows, :][3:4] * force
-
-    chain_forces(tables, weights, [(1, cells + 2)], emit, 13)
+    emit = add_kick(place, speed)
+    steps = [(own, own > 1, True) for own in range(1, cells - 1)]
+    carry = chain_forces(tables, weights, steps, emit, GROUP)
+    emit(cells - 1, force_of(tables, cells - 1, None, carry))
+
+
+def last_outer_kernel(
+    cells, edge_ref, occ_ref, place_ref, speed_ref, pos_ref, vel_ref,
+    place, speed, weights, left, right, moved,
+):
+    base = cells - 8
+    place[0:64, :] = place_ref[base * 8 : cells * 8, :]
+    speed[0:64, :] = speed_ref[base * 8 : cells * 8, :]
     for axis in range(3):
-        pos_ref[axis] = place[pl.ds(2 * 8 + axis, cells, stride=8), :]
-        vel_ref[axis] = speed[pl.ds(2 * 8 + axis, cells, stride=8), :]
+        for parity in range(2):
+            slot = (8 + parity) * 8 + axis
+            row = axis * 2 + parity
+            place[slot : slot + 1, :] = edge_ref[row : row + 1, :]
+            speed[slot : slot + 1, :] = edge_ref[row + 6 : row + 7, :]
+        slot = 10 * 8 + axis
+        place[slot : slot + 1, :] = edge_ref[12 + axis : 13 + axis, :]
+    for parity in range(2):
+        slot = (8 + parity) * 8 + 3
+        place[slot : slot + 1, :] = place_ref[
+            (cells + parity) * 8 + 3 : (cells + parity) * 8 + 4, :
+        ]
+    tables = (left, right, moved)
+    planes = [place[pl.ds(axis, 16, stride=8), :] for axis in range(3)]
+    occupied = jnp.concatenate(
+        [
+            jnp.zeros((7, LANES), F32),
+            occ_ref[cells - 3 : cells, :],
+            edge_ref[15:16, :],
+            jnp.zeros((5, LANES), F32),
+        ],
+        axis=0,
+    )
+    put_tables(planes, occupied, tables, 0)
+    steps = [(own, True, own < 9) for own in range(7, 10)]
+    chain_forces(tables, weights, steps, add_kick(place, speed), GROUP)
+    for axis in range(3):
+        for out_ref, whole, end in ((pos_ref, place_ref, place), (vel_ref, speed_ref, speed)):
+            out_ref[axis, 0 : base, :] = whole[pl.ds(2 * 8 + axis, base, stride=8), :]
+            out_ref[axis, base:cells, :] = end[pl.ds(2 * 8 + axis, 8, stride=8), :]
 
 
 def local(positions, velocities, counts, types, masses):
@@ -344,6 +401,9 @@
             out_specs=jax.tree.map(lambda _: VMEM, outs),
             scratch_shapes=scratches,
             compiler_params=PARAMS,
+            cost_estimate=pl.CostEstimate(
+                flops=20_000_000_000, bytes_accessed=1_000_000, transcendentals=0
+            ),
         )(*args)
 
     def shaped(*shape):
@@ -363,15 +423,37 @@
 
     pos = positions[0].transpose(1, 0, 2)
     vel = velocities[0].transpose(1, 0, 2)
-    slab_scratch = [scratch(rows * 8), scratch(rows * 8), scratch(rows), weight_scratch(rows)]
-    slab_scratch += [scratch(rows * ROWS)] * 3
-    edge = call(lambda *r: edge_kernel(cells, *r), shaped(32, LANES), [], pos, vel, occupied, kick)
+    window = shaped(rows * 8, LANES)
+    slab_scratch = [weight_scratch(cells)] + [scratch(rows * ROWS)] * 3
+    edge_scratch = [scratch(rows * 8)] * 2 + [weight_scratch(8)] + [scratch(16 * ROWS)] * 3
+    last = cells // 8 - 1
+    smem = pl.BlockSpec(memory_space=pltpu.SMEM)
+    edge = pl.pallas_call(
+        lambda *r: edge_kernel(cells, *r),
+        grid=(1,),
+        out_shape=shaped(32, LANES),
+        in_specs=[
+            smem,
+            smem,
+            pl.BlockSpec((3, 8, LANES), lambda i: (0, last, 0)),
+            pl.BlockSpec((3, 8, LANES), lambda i: (0, last, 0)),
+            pl.BlockSpec((8, LANES), lambda i: (last, 0)),
+        ],
+        out_specs=pl.BlockSpec((32, LANES), lambda i: (0, 0)),
+        compiler_params=PARAMS,
+    )(counts, masses, pos, vel, types)
     edge = slab_shift(edge, 1)
+    place, speed = call(
+        lambda *r: first_inner_kernel(cells, *r),
+        (window, window),
+        slab_scratch,
+        pos, vel, occupied, kick,
+    )
     send = call(
-        lambda *r: first_kernel(cells, *r),
+        lambda *r: first_outer_kernel(cells, *r),
         shaped(images * WIDE, LANES),
-        slab_scratch,
-        edge, pos, vel, occupied, kick,
+        edge_scratch,
+        edge, occupied, place, speed,
     )
     got = transpose(send)
     occ_wide = jnp.concatenate([edge[24:28], occupied], axis=0)
@@ -399,11 +481,17 @@
         axis=0,
     )
     message = slab_shift(message, -1)
+    place, speed = call(
+        lambda *r: last_inner_kernel(cells, *r),
+        (window, window),
+        [scratch(cells)] + slab_scratch,
+        got, edge, occupied, kick,
+    )
     pos, vel = call(
-        lambda *r: last_kernel(cells, *r),
+        lambda *r: last_outer_kernel(cells, *r),
         (shaped(*pos.shape), shaped(*vel.shape)),
-        slab_scratch,
-        got, message, edge, occupied, kick,
+        edge_scratch,
+        message, occupied, place, speed,
     )
     return pos.transpose(1, 0, 2)[None], vel.transpose(1, 0, 2)[None]
 

time: 99.7 us -> 99.6 us (level)
  local copies, waits for them, and re-layouts: 2.35 us -> 4.63 us
  waiting for transfers between devices: 45.8 us -> 43.7 us
  Pallas kernels: 16.3 us -> 17.4 us
    ppermute x2, waiting for transfers between devices: 8.13 us -> 1.35 us  [slab_shift(): return lax.ppermute(array, 'space', pairs)]
    all_to_all x2, waiting for transfers between devices: 37.7 us -> 42.4 us  [transpose(): lax.all_to_all(blocks, 'image', split_axis=0, concat_axis=0, tiled=True)]
    unnamed x18 -> x22, local copies, waits for them, and re-layouts: 0.94 us -> 3.23 us
    ppermute x2, starting transfers between devices: 12 us -> 9.77 us  [slab_shift(): return lax.ppermute(array, 'space', pairs)]
    all_to_all x2, starting transfers between devices: 21 us -> 22.4 us  [transpose(): lax.all_to_all(blocks, 'image', split_axis=0, concat_axis=0, tiled=True)]
    pallas_call x4 -> x5, Pallas kernels: 16.3 us -> 16.8 us  [call(): pl.pallas_call(kernel, out_shape=outs, in_specs=[VMEM] * len(args), out_s...]
  transfers between devices with their start and end apart: 4 -> 4, of which waited for: 4 -> 3; matrix products, arithmetic and copies ran while one was open for 0% -> 0% of each run, Pallas kernels for 0% -> 7%
where the time goes in v3:
time: 99.6 us; the launch traced here: 99 us
  waiting for transfers between devices  43.7 us (44%)
  starting transfers between devices  32.1 us (32%)
  Pallas kernels  17.4 us (17%)
  local copies, waits for them, and re-layouts  4.63 us (5%)
    all_to_all x2, waiting for transfers between devices, transpose(): lax.all_to_all(blocks, 'image', split_axis=0, concat_axis=0, tiled=True)  42.4 us
    all_to_all x2, starting transfers between devices, transpose(): lax.all_to_all(blocks, 'image', split_axis=0, concat_axis=0, tiled=True)  22.4 us
    pallas_call x5, Pallas kernels, call(): pl.pallas_call(kernel, out_shape=outs, in_specs=[VMEM] * len(args), out_s...  16.8 us
    ppermute x2, starting transfers between devices, slab_shift(): return lax.ppermute(array, 'space', pairs)  9.77 us
    unnamed x22, local copies, waits for them, and re-layouts  3.23 us
  transfers between devices with their start and end apart: 4, of which 3 were waited for; matrix products, arithmetic and copies ran while one was open for 0% of the time, Pallas kernels for 7%

profile of v3, /device:TPU:1, one launch (start us, length us, event | category | flops | bytes accessed | tf_op | source)
XLA Modules:
  0.0 99.0 jit_solution(18314526610260602919)
XLA Ops:
  0.6 0.0 copy-start.6
  0.6 0.0 copy-start.7
  0.7 0.6 copy-done.6
  1.3 0.0 copy-done.7
  1.3 0.0 copy-start
  1.3 0.8 copy-done
  2.1 0.0 copy-start.3
  2.1 0.9 copy-done.3
  3.0 0.0 copy-start.5
  3.0 0.9 copy-done.5
  3.8 0.6 shard_map.77
  4.4 0.0 copy-start.4
  4.4 4.7 %collective-permute-start = (f32[32,128]{1,0:T(8,128)S(1)}, f32[32,128]{1,0:T(8,128)S(1)}, u32[]{:S(2)}, u32[]{:S(2)}) collective-permute-start(f32[32,128]{1,0:T(8,128)S(1)} %shard_map.77), channel_id=1, source_target_pairs={{0,1},{1,2},{2,3},{3,4},{4,5},{5,6},{6,7},{7,8},{8,9},{9,10},{10,1... | collective-permute-start | bytes 49160 | tf_op jit(solution)/shard_map/ppermute | solution.py:389
  9.2 0.1 select_reduce_fusion
  9.2 0.1 fusion.r_2_.r_1_
  9.3 0.0 copy-start.1
  9.3 0.0 copy-done.4
  9.4 3.3 %shard_map.78 = (f32[576,128]{1,0:T(8,128)S(1)}, f32[576,128]{1,0:T(8,128)S(1)}) custom-call(f32[3,64,128]{2,1,0:T(8,128)S(1)} %bitcast.20, f32[3,64,128]{2,1,0:T(8,128)S(1)} %bitcast.22, f32[64,128]{1,0:T(8,128)S(1)} %fusion.r_2_.r_1_, f32[64,128]{1,0:T(8,128)S(1)} %divide_multiply_fusion.r_3_), custom_call_target="tpu_custom_call" | custom-call | flops 20000000000 | bytes 1000000 | tf_op jit(solution)/shard_map/pallas_call | solution.py:397
  12.7 1.4 %collective-permute-done.r_0_.r_1_ = f32[32,128]{1,0:T(8,128)S(1)} collective-permute-done((f32[32,128]{1,0:T(8,128)S(1)}, f32[32,128]{1,0:T(8,128)S(1)}, u32[]{:S(2)}, u32[]{:S(2)}) %collective-permute-start) | collective-permute-done | bytes 16416 | tf_op jit(solution)/shard_map/ppermute | solution.py:389
  14.0 0.0 copy-start.8
  14.0 1.4 %shard_map.79 = f32[768,128]{1,0:T(8,128)} custom-call(f32[32,128]{1,0:T(8,128)S(1)} %collective-permute-done.r_0_.r_1_, f32[64,128]{1,0:T(8,128)S(1)} %fusion.r_2_.r_1_, f32[576,128]{1,0:T(8,128)S(1)} %get-tuple-element.8.r_2_, f32[576,128]{1,0:T(8,128)S(1)} %get-tuple-element.9.r_3_), custom_call_target="tpu_custom_call" | custom-call | flops 20000000000 | bytes 1000000 | tf_op jit(solution)/shard_map/pallas_call | solution.py:397
  15.4 16.3 %all-to-all-start = ((f32[32,6,4,128]{3,2,1,0:T(4,128)}), f32[32,6,4,128]{3,2,1,0:T(4,128)S(1)}, u32[]{:S(2)}, u32[]{:S(2)}) async-start(f32[32,6,4,128]{3,2,1,0:T(4,128)} %bitcast.6), calls=%async_computation | async-start | bytes 786432 | tf_op jit(solution)/shard_map/all_to_all | solution.py:393
  31.8 0.1 pad.2.clone
  31.8 0.0 copy-done.8
  31.8 0.0 slice-start.1
  31.8 0.0 copy-start.10
  31.9 0.6 slice-done.1
  32.5 0.1 maximum_maximum_fusion.r_1_
  32.6 25.1 %all-to-all-done = f32[32,6,4,128]{3,2,1,0:T(4,128)S(1)} async-done(((f32[32,6,4,128]{3,2,1,0:T(4,128)}), f32[32,6,4,128]{3,2,1,0:T(4,128)S(1)}, u32[]{:S(2)}, u32[]{:S(2)}) %all-to-all-start) | async-done | bytes 393248 | tf_op jit(solution)/shard_map/all_to_all | solution.py:393
  57.7 0.0 copy-done.10
  57.7 7.7 %shard_map.80 = f32[384,128]{1,0:T(8,128)} custom-call(f32[64,64]{1,0:T(8,128)S(1)} %copy-done.10, f32[8,128]{1,0:T(8,128)S(1)} %maximum_maximum_fusion.r_1_, f32[768,128]{1,0:T(8,128)S(1)} %bitcast.16), custom_call_target="tpu_custom_call" | custom-call | flops 20000000000 | bytes 1000000 | tf_op jit(solution)/shard_map/pallas_call | solution.py:397
  65.5 6.0 %all-to-all-start.1 = ((f32[32,3,4,128]{3,2,1,0:T(4,128)}), f32[32,3,4,128]{3,2,1,0:T(4,128)S(1)}, u32[]{:S(2)}, u32[]{:S(2)}) async-start(f32[32,3,4,128]{3,2,1,0:T(4,128)} %bitcast.8), calls=%async_computation.1 | async-start | bytes 393216 | tf_op jit(solution)/shard_map/all_to_all | solution.py:393
  71.5 0.0 copy-done.1
  71.5 0.0 copy-start.2
  71.5 17.2 %all-to-all-done.1 = f32[32,3,4,128]{3,2,1,0:T(4,128)S(1)} async-done(((f32[32,3,4,128]{3,2,1,0:T(4,128)}), f32[32,3,4,128]{3,2,1,0:T(4,128)S(1)}, u32[]{:S(2)}, u32[]{:S(2)}) %all-to-all-start.1) | async-done | bytes 196640 | tf_op jit(solution)/shard_map/all_to_all | solution.py:393
  88.8 0.0 slice-start
  88.8 0.0 copy-start.9
  88.8 0.6 slice-done
  89.5 5.0 %collective-permute-start.1 = (f32[16,128]{1,0:T(8,128)S(1)}, f32[16,128]{1,0:T(8,128)S(1)}, u32[]{:S(2)}, u32[]{:S(2)}) collective-permute-start(f32[16,128]{1,0:T(8,128)S(1)} %concatenate.15), channel_id=1, source_target_pairs={{0,15},{1,0},{2,1},{3,2},{4,3},{5,4},{6,5},{7,6},{8,7},{9,8},{10,9... | collective-permute-start | bytes 24584 | tf_op jit(solution)/shard_map/ppermute | solution.py:389
  94.5 0.0 copy-done.2
  94.5 0.0 copy-done.9
  94.5 3.3 %shard_map.81 = (f32[576,128]{1,0:T(8,128)S(1)}, f32[576,128]{1,0:T(8,128)S(1)}) custom-call(f32[384,128]{1,0:T(8,128)S(1)} %bitcast.18, f32[32,128]{1,0:T(8,128)S(1)} %copy-done.9, f32[64,128]{1,0:T(8,128)S(1)} %copy-done.2, f32[64,128]{1,0:T(8,128)S(1)} %divide_multiply_fusion.r_3_), custom_call_target="tpu_custom_call" | custom-call | flops 20000000000 | bytes 1000000 | tf_op jit(solution)/shard_map/pallas_call | solution.py:397
  97.9 0.0 collective-permute-done.1.r_0_
  97.9 1.1 %shard_map.82 = (f32[3,64,128]{2,1,0:T(8,128)}, f32[3,64,128]{2,1,0:T(8,128)}) custom-call(f32[16,128]{1,0:T(8,128)S(1)} %collective-permute-done.1.r_0_, f32[64,128]{1,0:T(8,128)S(1)} %copy-done.2, f32[576,128]{1,0:T(8,128)S(1)} %get-tuple-element.10.r_2_, f32[576,128]{1,0:T(8,128)S(1)} %get-tuple-element.11.r_3_), custom_call_target="tpu_custom_call" | custom-call | flops 20000000000 | bytes 1000000 | tf_op jit(solution)/shard_map/pallas_call | solution.py:397
  (9 shorter events, 0.1 us)
Async XLA Ops:
  0.6 0.7 copy-start.6
  0.6 0.7 copy-start.7
  1.3 0.8 copy-start
  2.1 0.9 copy-start.3
  3.0 0.9 copy-start.5
  4.4 4.9 %copy-start.4 = (f32[1,64,3,128]{3,1,2,0:T(8,128)S(1)}, f32[1,64,3,128]{3,1,2,0:T(8,128)}, u32[]{:S(2)}) copy-start(f32[1,64,3,128]{3,1,2,0:T(8,128)} %param.6) | copy-start | bytes 294916
  4.4 9.6 %collective-permute-start = (f32[32,128]{1,0:T(8,128)S(1)}, f32[32,128]{1,0:T(8,128)S(1)}, u32[]{:S(2)}, u32[]{:S(2)}) collective-permute-start(f32[32,128]{1,0:T(8,128)S(1)} %shard_map.77), channel_id=1, source_target_pairs={{0,1},{1,2},{2,3},{3,4},{4,5},{5,6},{6,7},{7,8},{8,9},{9,10},{10,1... | collective-permute-start | bytes 49160 | tf_op jit(solution)/shard_map/ppermute | solution.py:389
  9.3 62.2 %copy-start.1 = (f32[64,128]{1,0:T(8,128)}, f32[64,128]{1,0:T(8,128)S(1)}, u32[]{:S(2)}) copy-start(f32[64,128]{1,0:T(8,128)S(1)} %fusion.r_2_.r_1_) | copy-start | bytes 98308
  14.0 17.8 %copy-start.8 = (f32[32,128]{1,0:T(8,128)}, f32[32,128]{1,0:T(8,128)S(1)}, u32[]{:S(2)}) copy-start(f32[32,128]{1,0:T(8,128)S(1)} %collective-permute-done.r_0_.r_1_) | copy-start | bytes 49156
  15.4 42.4 %all-to-all-start = ((f32[32,6,4,128]{3,2,1,0:T(4,128)}), f32[32,6,4,128]{3,2,1,0:T(4,128)S(1)}, u32[]{:S(2)}, u32[]{:S(2)}) async-start(f32[32,6,4,128]{3,2,1,0:T(4,128)} %bitcast.6), calls=%async_computation | async-start | bytes 786432 | tf_op jit(solution)/shard_map/all_to_all | solution.py:393
  31.8 0.7 slice-start.1
  31.8 25.9 %copy-start.10 = (f32[64,64]{1,0:T(8,128)S(1)}, f32[64,64]{1,0:T(8,128)}, u32[]{:S(2)}) copy-start(f32[64,64]{1,0:T(8,128)} %constant.49.clone.r_0_) | copy-start | bytes 49156
  65.5 23.3 %all-to-all-start.1 = ((f32[32,3,4,128]{3,2,1,0:T(4,128)}), f32[32,3,4,128]{3,2,1,0:T(4,128)S(1)}, u32[]{:S(2)}, u32[]{:S(2)}) async-start(f32[32,3,4,128]{3,2,1,0:T(4,128)} %bitcast.8), calls=%async_computation.1 | async-start | bytes 393216 | tf_op jit(solution)/shard_map/all_to_all | solution.py:393
  71.5 23.0 %copy-start.2 = (f32[64,128]{1,0:T(8,128)S(1)}, f32[64,128]{1,0:T(8,128)}, u32[]{:S(2)}) copy-start(f32[64,128]{1,0:T(8,128)} %copy-done.1) | copy-start | bytes 98308
  88.8 0.7 slice-start
  88.8 5.7 %copy-start.9 = (f32[32,128]{1,0:T(8,128)S(1)}, f32[32,128]{1,0:T(8,128)}, u32[]{:S(2)}) copy-start(f32[32,128]{1,0:T(8,128)} %copy-done.8) | copy-start | bytes 49156
  89.5 8.4 %collective-permute-start.1 = (f32[16,128]{1,0:T(8,128)S(1)}, f32[16,128]{1,0:T(8,128)S(1)}, u32[]{:S(2)}, u32[]{:S(2)}) collective-permute-start(f32[16,128]{1,0:T(8,128)S(1)} %concatenate.15), channel_id=1, source_target_pairs={{0,15},{1,0},{2,1},{3,2},{4,3},{5,4},{6,5},{7,6},{8,7},{9,8},{10,9... | collective-permute-start | bytes 24584 | tf_op jit(solution)/shard_map/ppermute | solution.py:389

commit v4 on v3

--- a/solution.py
+++ b/solution.py
@@ -54,42 +54,42 @@
     return high, mid, low
 
 
-def put_tables(planes, occupied, tables, start, stride=1):
+def put_tables(planes, occupied, tables, start, sides="lrm"):
     left, right, moved = tables
     count = planes[0].shape[0]
     one = jnp.ones_like(planes[0])
 
     def put(ref, row, value):
-        ref[pl.ds(start * ROWS + row, count, stride=stride * ROWS), :] = value
+        ref[pl.ds(start * ROWS + row, count, stride=ROWS), :] = value
 
     def norm(parts):
         total = parts[0] * parts[0] + parts[1] * parts[1] + parts[2] * parts[2]
         return split3(-0.5 * total - FAR * (1.0 - occupied))
 
+    def put_right(ref, pieces, norms):
+        for axis in range(3):
+            high, mid, low = pieces[axis]
+            for row, value in ((0, high), (4, high), (8, mid), (12, high), (16, low), (20, mid)):
+                put(ref, row + axis, value)
+        for piece in range(3):
+            put(ref, 8 * piece + 3, one)
+            put(ref, 8 * piece + 7, norms[piece])
+
     scaled = [ALPHA * plane for plane in planes]
     pieces = [split3(part) for part in scaled]
-    norms = norm(scaled)
-    for axis in range(3):
-        high, mid, low = pieces[axis]
-        for row, value in ((0, high), (4, mid), (8, high), (12, low), (16, high), (20, mid)):
-            put(left, row + axis, value)
-        for row, value in ((0, high), (4, high), (8, mid), (12, high), (16, low), (20, mid)):
-            put(right, row + axis, value)
-            if axis:
-                put(moved, row + axis, value)
-    for piece in range(3):
-        put(left, 8 * piece + 3, norms[piece])
-        put(left, 8 * piece + 7, one)
-        put(right, 8 * piece + 3, one)
-        put(right, 8 * piece + 7, norms[piece])
-        put(moved, 8 * piece + 3, one)
-    ahead = ALPHA * (planes[0] + 1.0)
-    high, mid, low = split3(ahead)
-    for row, value in ((0, high), (4, high), (8, mid), (12, high), (16, low), (20, mid)):
-        put(moved, row, value)
-    norms = norm([ahead, scaled[1], scaled[2]])
-    for piece in range(3):
-        put(moved, 8 * piece + 7, norms[piece])
+    if "l" in sides:
+        norms = norm(scaled)
+        for axis in range(3):
+            high, mid, low = pieces[axis]
+            for row, value in ((0, high), (4, mid), (8, high), (12, low), (16, high), (20, mid)):
+                put(left, row + axis, value)
+        for piece in range(3):
+            put(left, 8 * piece + 3, norms[piece])
+            put(left, 8 * piece + 7, one)
+        put_right(right, pieces, norms)
+    if "m" in sides:
+        ahead = ALPHA * (planes[0] + 1.0)
+        put_right(moved, [split3(ahead)] + pieces[1:], norm([ahead, scaled[1], scaled[2]]))
 
 
 def table_rows(ref, cell):
@@ -154,15 +154,15 @@
     return GAIN * total
 
 
-def chain_forces(tables, weights, steps, emit, group):
+def chain_forces(tables, weights, steps, emit, group, ahead=1):
     carry = None
     for start in range(0, len(steps), group):
         part = list(enumerate(steps))[start : start + group]
         for index, (own, inner, _) in part:
-            put_weights(tables, weights, index, own, own + 1, inner)
+            put_weights(tables, weights, index, own, own + ahead, inner)
         for index, (own, inner, more) in part:
             if inner:
-                sums = own_sums(tables, weights, index, own, own + 1)
+                sums = own_sums(tables, weights, index, own, own + ahead)
                 emit(own, force_of(tables, own, sums, carry))
             carry = next_sums(tables, weights, index, own) if more else None
     return carry
@@ -284,22 +284,24 @@
         source, first = ((outer, 0), (inner, 0), (inner, 3), (outer, 3))[slot]
         planes = [lanes_of(source, first + axis)[:images] for axis in range(3)]
         occupied = jnp.broadcast_to(info_ref[slot : slot + 1, :], (images, LANES))
-        put_tables(planes, occupied, tables, slot, stride=4)
+        put_tables(planes, occupied, tables, slot * images, ("lr", "lrm", "lrm", "m")[slot])
 
     def emit(cell, force):
-        row = (cell // 4 * 2 + cell % 4 - 1) * 8
+        row = (cell - images) * 8
         forces[row : row + 8, :] = force
 
     steps = [
-        (4 * image + slot, slot > 0, slot < 2) for image in range(images) for slot in range(3)
+        (slot * images + image, slot > 0, slot < 2)
+        for image in range(images)
+        for slot in range(3)
     ]
-    chain_forces(tables, weights, steps, emit, GROUP)
+    chain_forces(tables, weights, steps, emit, 12, ahead=images)
     blocks = []
     for parity in range(2):
         kick = 2.0 * info_ref[4 + parity : 5 + parity, :]
         for axis in range(3):
             now = lanes_of(inner, parity * 3 + axis)
-            force = forces[pl.ds(parity * 8 + axis, images, stride=16), :]
+            force = forces[pl.ds(parity * images * 8 + axis, images, stride=8), :]
             blocks.append(jnp.concatenate([now[:images], now[images:] + kick * force], axis=0))
     ahead = cycle(matrix_ref[...], blocks)
     for parity in range(2):
@@ -440,7 +442,7 @@
             pl.BlockSpec((8, LANES), lambda i: (last, 0)),
         ],
         out_specs=pl.BlockSpec((32, LANES), lambda i: (0, 0)),
-        compiler_params=PARAMS,
+        compiler_params=pltpu.CompilerParams(vmem_limit_bytes=62 * 1024 * 1024),
     )(counts, masses, pos, vel, types)
     edge = slab_shift(edge, 1)
     place, speed = call(

time: 99.6 us -> 94.4 us (0.948)
  local copies, waits for them, and re-layouts: 4.63 us -> 1.45 us
  Pallas kernels: 17.4 us -> 15.8 us
  waiting for transfers between devices: 43.7 us -> 42.5 us
  starting transfers between devices: 32.1 us -> 33.1 us
    unnamed x22 -> x20, local copies, waits for them, and re-layouts: 3.23 us -> 0.04 us
    pallas_call x5, Pallas kernels: 16.8 us -> 14.3 us  [call(): pl.pallas_call(kernel, out_shape=outs, in_specs=[VMEM] * len(args), out_s...]
    all_to_all x2, waiting for transfers between devices: 42.4 us -> 40.9 us  [transpose(): lax.all_to_all(blocks, 'image', split_axis=0, concat_axis=0, tiled=True)]
    ppermute x2, starting transfers between devices: 9.77 us -> 10.9 us  [slab_shift(): return lax.ppermute(array, 'space', pairs)]
where the time goes in v4:
time: 94.4 us; the launch traced here: 94 us
  waiting for transfers between devices  42.5 us (45%)
  starting transfers between devices  33.1 us (35%)
  Pallas kernels  15.8 us (17%)
  local copies, waits for them, and re-layouts  1.45 us (2%)
    all_to_all x2, waiting for transfers between devices, transpose(): lax.all_to_all(blocks, 'image', split_axis=0, concat_axis=0, tiled=True)  40.9 us
    all_to_all x2, starting transfers between devices, transpose(): lax.all_to_all(blocks, 'image', split_axis=0, concat_axis=0, tiled=True)  22.3 us
    pallas_call x5, Pallas kernels, call(): pl.pallas_call(kernel, out_shape=outs, in_specs=[VMEM] * len(args), out_s...  14.3 us
    ppermute x2, starting transfers between devices, slab_shift(): return lax.ppermute(array, 'space', pairs)  10.9 us
  transfers between devices with their start and end apart: 4, of which 3 were waited for; matrix products, arithmetic and copies ran while one was open for 0% of the time, Pallas kernels for 7%

profile of v4, /device:TPU:1, one launch (start us, length us, event | category | flops | bytes accessed | tf_op | source)
XLA Modules:
  0.0 94.0 jit_solution(12065051799692432226)
XLA Ops:
  0.6 0.0 copy-start.7
  0.6 0.0 copy-start.8
  0.7 0.0 copy-start.9
  0.7 0.0 copy-start.3
  0.7 1.4 %shard_map.77 = f32[32,128]{1,0:T(8,128)} custom-call(s32[64]{0:T(128)} %r_0_.2, f32[4]{0:T(128)} %r_1_.1, f32[3,64,128]{2,1,0:T(8,128)} %bitcast.19, f32[3,64,128]{2,1,0:T(8,128)} %bitcast.21, s32[64,128]{1,0:T(8,128)} %r_4_.1), custom_call_target="tpu_custom_call" | custom-call | tf_op jit(solution)/shard_map/pallas_call | solution.py:433
  2.1 0.0 copy-start.2
  2.1 4.7 %collective-permute-start = (f32[32,128]{1,0:T(8,128)}, f32[32,128]{1,0:T(8,128)S(1)}, u32[]{:S(2)}, u32[]{:S(2)}) collective-permute-start(f32[32,128]{1,0:T(8,128)} %shard_map.77), channel_id=1, source_target_pairs={{0,1},{1,2},{2,3},{3,4},{4,5},{5,6},{6,7},{7,8},{8,9},{9,10},{10,1... | collective-permute-start | bytes 49160 | tf_op jit(solution)/shard_map/ppermute | solution.py:391
  6.8 0.0 copy-done.7
  6.8 0.0 copy-done.8
  6.8 0.1 select_reduce_fusion
  6.9 0.0 copy-done.9
  6.9 0.1 fusion.r_2_.r_1_
  7.0 0.0 copy-start
  7.0 0.0 copy-done.3
  7.1 0.0 copy-done.2
  7.1 3.3 %shard_map.78 = (f32[576,128]{1,0:T(8,128)S(1)}, f32[576,128]{1,0:T(8,128)S(1)}) custom-call(f32[3,64,128]{2,1,0:T(8,128)S(1)} %bitcast.20, f32[3,64,128]{2,1,0:T(8,128)S(1)} %bitcast.22, f32[64,128]{1,0:T(8,128)S(1)} %fusion.r_2_.r_1_, f32[64,128]{1,0:T(8,128)S(1)} %divide_multiply_fusion.r_3_), custom_call_target="tpu_custom_call" | custom-call | flops 20000000000 | bytes 1000000 | tf_op jit(solution)/shard_map/pallas_call | solution.py:399
  10.4 1.5 %collective-permute-done.r_0_.r_1_ = f32[32,128]{1,0:T(8,128)S(1)} collective-permute-done((f32[32,128]{1,0:T(8,128)}, f32[32,128]{1,0:T(8,128)S(1)}, u32[]{:S(2)}, u32[]{:S(2)}) %collective-permute-start) | collective-permute-done | bytes 16416 | tf_op jit(solution)/shard_map/ppermute | solution.py:391
  11.9 0.0 copy-start.4
  11.9 1.4 %shard_map.79 = f32[768,128]{1,0:T(8,128)} custom-call(f32[32,128]{1,0:T(8,128)S(1)} %collective-permute-done.r_0_.r_1_, f32[64,128]{1,0:T(8,128)S(1)} %fusion.r_2_.r_1_, f32[576,128]{1,0:T(8,128)S(1)} %get-tuple-element.8.r_2_, f32[576,128]{1,0:T(8,128)S(1)} %get-tuple-element.9.r_3_), custom_call_target="tpu_custom_call" | custom-call | flops 20000000000 | bytes 1000000 | tf_op jit(solution)/shard_map/pallas_call | solution.py:399
  13.3 16.1 %all-to-all-start = ((f32[32,6,4,128]{3,2,1,0:T(4,128)}), f32[32,6,4,128]{3,2,1,0:T(4,128)S(1)}, u32[]{:S(2)}, u32[]{:S(2)}) async-start(f32[32,6,4,128]{3,2,1,0:T(4,128)} %bitcast.6), calls=%async_computation | async-start | bytes 786432 | tf_op jit(solution)/shard_map/all_to_all | solution.py:395
  29.4 0.1 pad.2.clone
  29.5 0.0 copy-done.4
  29.5 0.0 slice-start.1
  29.5 0.0 copy-start.6
  29.6 0.6 slice-done.1
  30.2 0.1 maximum_maximum_fusion.r_1_
  30.3 24.6 %all-to-all-done = f32[32,6,4,128]{3,2,1,0:T(4,128)S(1)} async-done(((f32[32,6,4,128]{3,2,1,0:T(4,128)}), f32[32,6,4,128]{3,2,1,0:T(4,128)S(1)}, u32[]{:S(2)}, u32[]{:S(2)}) %all-to-all-start) | async-done | bytes 393248 | tf_op jit(solution)/shard_map/all_to_all | solution.py:395
  54.9 0.0 copy-done.6
  54.9 5.3 %shard_map.80 = f32[384,128]{1,0:T(8,128)} custom-call(f32[64,64]{1,0:T(8,128)S(1)} %copy-done.6, f32[8,128]{1,0:T(8,128)S(1)} %maximum_maximum_fusion.r_1_, f32[768,128]{1,0:T(8,128)S(1)} %bitcast.16), custom_call_target="tpu_custom_call" | custom-call | flops 20000000000 | bytes 1000000 | tf_op jit(solution)/shard_map/pallas_call | solution.py:399
  60.1 6.1 %all-to-all-start.1 = ((f32[32,3,4,128]{3,2,1,0:T(4,128)}), f32[32,3,4,128]{3,2,1,0:T(4,128)S(1)}, u32[]{:S(2)}, u32[]{:S(2)}) async-start(f32[32,3,4,128]{3,2,1,0:T(4,128)} %bitcast.8), calls=%async_computation.1 | async-start | bytes 393216 | tf_op jit(solution)/shard_map/all_to_all | solution.py:395
  66.3 0.0 copy-done
  66.3 0.0 copy-start.1
  66.3 16.3 %all-to-all-done.1 = f32[32,3,4,128]{3,2,1,0:T(4,128)S(1)} async-done(((f32[32,3,4,128]{3,2,1,0:T(4,128)}), f32[32,3,4,128]{3,2,1,0:T(4,128)S(1)}, u32[]{:S(2)}, u32[]{:S(2)}) %all-to-all-start.1) | async-done | bytes 196640 | tf_op jit(solution)/shard_map/all_to_all | solution.py:395
  82.7 0.0 slice-start
  82.7 0.0 copy-start.5
  82.7 0.6 slice-done
  83.3 6.2 %collective-permute-start.1 = (f32[16,128]{1,0:T(8,128)S(1)}, f32[16,128]{1,0:T(8,128)S(1)}, u32[]{:S(2)}, u32[]{:S(2)}) collective-permute-start(f32[16,128]{1,0:T(8,128)S(1)} %concatenate.15), channel_id=1, source_target_pairs={{0,15},{1,0},{2,1},{3,2},{4,3},{5,4},{6,5},{7,6},{8,7},{9,8},{10,9... | collective-permute-start | bytes 24584 | tf_op jit(solution)/shard_map/ppermute | solution.py:391
  89.5 0.0 copy-done.1
  89.5 0.0 copy-done.5
  89.5 3.3 %shard_map.81 = (f32[576,128]{1,0:T(8,128)S(1)}, f32[576,128]{1,0:T(8,128)S(1)}) custom-call(f32[384,128]{1,0:T(8,128)S(1)} %bitcast.18, f32[32,128]{1,0:T(8,128)S(1)} %copy-done.5, f32[64,128]{1,0:T(8,128)S(1)} %copy-done.1, f32[64,128]{1,0:T(8,128)S(1)} %divide_multiply_fusion.r_3_), custom_call_target="tpu_custom_call" | custom-call | flops 20000000000 | bytes 1000000 | tf_op jit(solution)/shard_map/pallas_call | solution.py:399
  92.9 0.0 collective-permute-done.1.r_0_
  92.9 1.1 %shard_map.82 = (f32[3,64,128]{2,1,0:T(8,128)}, f32[3,64,128]{2,1,0:T(8,128)}) custom-call(f32[16,128]{1,0:T(8,128)S(1)} %collective-permute-done.1.r_0_, f32[64,128]{1,0:T(8,128)S(1)} %copy-done.1, f32[576,128]{1,0:T(8,128)S(1)} %get-tuple-element.10.r_2_, f32[576,128]{1,0:T(8,128)S(1)} %get-tuple-element.11.r_3_), custom_call_target="tpu_custom_call" | custom-call | flops 20000000000 | bytes 1000000 | tf_op jit(solution)/shard_map/pallas_call | solution.py:399
  (9 shorter events, 0.1 us)
Async XLA Ops:
  0.6 6.2 %copy-start.7 = (s32[64,128]{1,0:T(8,128)S(1)}, s32[64,128]{1,0:T(8,128)}, u32[]{:S(2)}) copy-start(s32[64,128]{1,0:T(8,128)} %r_4_.1) | copy-start | bytes 98308
  0.6 6.2 %copy-start.8 = (f32[4]{0:T(128)S(1)}, f32[4]{0:T(128)}, u32[]{:S(2)}) copy-start(f32[4]{0:T(128)} %r_1_.1) | copy-start | bytes 52
  0.7 6.3 %copy-start.9 = (s32[64]{0:T(128)S(1)}, s32[64]{0:T(128)}, u32[]{:S(2)}) copy-start(s32[64]{0:T(128)} %r_0_.2) | copy-start | bytes 772
  0.7 6.4 %copy-start.3 = (f32[1,64,3,128]{3,1,2,0:T(8,128)S(1)}, f32[1,64,3,128]{3,1,2,0:T(8,128)}, u32[]{:S(2)}) copy-start(f32[1,64,3,128]{3,1,2,0:T(8,128)} %param.7) | copy-start | bytes 294916
  2.1 5.0 %copy-start.2 = (f32[1,64,3,128]{3,1,2,0:T(8,128)S(1)}, f32[1,64,3,128]{3,1,2,0:T(8,128)}, u32[]{:S(2)}) copy-start(f32[1,64,3,128]{3,1,2,0:T(8,128)} %param.6) | copy-start | bytes 294916
  2.1 9.8 %collective-permute-start = (f32[32,128]{1,0:T(8,128)}, f32[32,128]{1,0:T(8,128)S(1)}, u32[]{:S(2)}, u32[]{:S(2)}) collective-permute-start(f32[32,128]{1,0:T(8,128)} %shard_map.77), channel_id=1, source_target_pairs={{0,1},{1,2},{2,3},{3,4},{4,5},{5,6},{6,7},{7,8},{8,9},{9,10},{10,1... | collective-permute-start | bytes 49160 | tf_op jit(solution)/shard_map/ppermute | solution.py:391
  7.0 59.3 %copy-start = (f32[64,128]{1,0:T(8,128)}, f32[64,128]{1,0:T(8,128)S(1)}, u32[]{:S(2)}) copy-start(f32[64,128]{1,0:T(8,128)S(1)} %fusion.r_2_.r_1_) | copy-start | bytes 98308
  11.9 17.6 %copy-start.4 = (f32[32,128]{1,0:T(8,128)}, f32[32,128]{1,0:T(8,128)S(1)}, u32[]{:S(2)}) copy-start(f32[32,128]{1,0:T(8,128)S(1)} %collective-permute-done.r_0_.r_1_) | copy-start | bytes 49156
  13.3 41.6 %all-to-all-start = ((f32[32,6,4,128]{3,2,1,0:T(4,128)}), f32[32,6,4,128]{3,2,1,0:T(4,128)S(1)}, u32[]{:S(2)}, u32[]{:S(2)}) async-start(f32[32,6,4,128]{3,2,1,0:T(4,128)} %bitcast.6), calls=%async_computation | async-start | bytes 786432 | tf_op jit(solution)/shard_map/all_to_all | solution.py:395
  29.5 0.7 slice-start.1
  29.5 25.3 %copy-start.6 = (f32[64,64]{1,0:T(8,128)S(1)}, f32[64,64]{1,0:T(8,128)}, u32[]{:S(2)}) copy-start(f32[64,64]{1,0:T(8,128)} %constant.49.clone.r_0_) | copy-start | bytes 49156
  60.1 22.5 %all-to-all-start.1 = ((f32[32,3,4,128]{3,2,1,0:T(4,128)}), f32[32,3,4,128]{3,2,1,0:T(4,128)S(1)}, u32[]{:S(2)}, u32[]{:S(2)}) async-start(f32[32,3,4,128]{3,2,1,0:T(4,128)} %bitcast.8), calls=%async_computation.1 | async-start | bytes 393216 | tf_op jit(solution)/shard_map/all_to_all | solution.py:395
  66.3 23.2 %copy-start.1 = (f32[64,128]{1,0:T(8,128)S(1)}, f32[64,128]{1,0:T(8,128)}, u32[]{:S(2)}) copy-start(f32[64,128]{1,0:T(8,128)} %copy-done) | copy-start | bytes 98308
  82.7 0.7 slice-start
  82.7 6.9 %copy-start.5 = (f32[32,128]{1,0:T(8,128)S(1)}, f32[32,128]{1,0:T(8,128)}, u32[]{:S(2)}) copy-start(f32[32,128]{1,0:T(8,128)} %copy-done.4) | copy-start | bytes 49156
  83.3 9.5 %collective-permute-start.1 = (f32[16,128]{1,0:T(8,128)S(1)}, f32[16,128]{1,0:T(8,128)S(1)}, u32[]{:S(2)}, u32[]{:S(2)}) collective-permute-start(f32[16,128]{1,0:T(8,128)S(1)} %concatenate.15), channel_id=1, source_target_pairs={{0,15},{1,0},{2,1},{3,2},{4,3},{5,4},{6,5},{7,6},{8,7},{9,8},{10,9... | collective-permute-start | bytes 24584 | tf_op jit(solution)/shard_map/ppermute | solution.py:391

commit v5 on v4

--- a/solution.py
+++ b/solution.py
@@ -2,6 +2,7 @@
 
 import jax
 import jax.numpy as jnp
+import ml_dtypes
 import numpy as np
 from jax import lax
 from jax.experimental import pallas as pl
@@ -43,7 +44,10 @@
     same = (table * np.cos(angle)) @ table.T
     from_velocity = (table * to_position) @ table.T
     from_position = (table * (-omega * np.sin(angle))) @ table.T
-    return np.block([[same, from_velocity], [from_position, same]]).astype(np.float32)
+    matrix = np.block([[same, from_velocity], [from_position, same]])
+    high = matrix.astype(ml_dtypes.bfloat16)
+    low = (matrix - high.astype(np.float64)).astype(ml_dtypes.bfloat16)
+    return np.concatenate([high, high, low], axis=1)
 
 
 def split3(value):
@@ -248,11 +252,11 @@
 
 
 def cycle(matrix, blocks):
+    state = jnp.concatenate(blocks, axis=1)
+    high = state.astype(BF16)
+    low = (state - high.astype(F32)).astype(BF16)
     return jnp.dot(
-        matrix,
-        jnp.concatenate(blocks, axis=1),
-        precision=lax.Precision.HIGHEST,
-        preferred_element_type=F32,
+        matrix, jnp.concatenate([high, low, high], axis=0), preferred_element_type=F32
     )
 
 
@@ -464,7 +468,8 @@
         [
             lax.dynamic_slice_in_dim(occ_wide, 2 * block + 1, 4, 0),
             lax.dynamic_slice_in_dim(kick_wide, 2 * block + 1, 2, 0),
-            jnp.zeros((2, LANES), F32),
+            occupied[0:1],
+            jnp.zeros((1, LANES), F32),
         ],
         axis=0,
     )
@@ -479,7 +484,7 @@
     message = jnp.concatenate(
         [got[0:SPAN]]
         + [got[chunk + 2 * axis : chunk + 2 * axis + 1] for axis in range(3)]
-        + [occupied[0:1]],
+        + [info[6:7]],
         axis=0,
     )
     message = slab_shift(message, -1)

time: 94.4 us -> 92.4 us (0.979)
  blocking collectives: 0 us -> 22.3 us
  waiting for transfers between devices: 42.5 us -> 26.1 us
  starting transfers between devices: 33.1 us -> 27 us
  Pallas kernels: 15.8 us -> 14.6 us
    all_to_all x0 -> x1, blocking collectives: none -> 22.3 us  [transpose(): lax.all_to_all(blocks, 'image', split_axis=0, concat_axis=0, tiled=True)]
    all_to_all x2 -> x1, waiting for transfers between devices: 40.9 us -> 24.5 us  [transpose(): lax.all_to_all(blocks, 'image', split_axis=0, concat_axis=0, tiled=True)]
    all_to_all x2 -> x1, starting transfers between devices: 22.3 us -> 16.1 us  [transpose(): lax.all_to_all(blocks, 'image', split_axis=0, concat_axis=0, tiled=True)]
    pallas_call x5, Pallas kernels: 14.3 us -> 13.2 us  [call(): pl.pallas_call(kernel, out_shape=outs, in_specs=[VMEM] * len(args), out_s...]
  transfers between devices with their start and end apart: 4 -> 3, of which waited for: 3 -> 2; matrix products, arithmetic and copies ran while one was open for 0% -> 0% of each run, Pallas kernels for 7% -> 7%
where the time goes in v5:
time: 92.4 us; the launch traced here: 92 us
  starting transfers between devices  27 us (29%)
  waiting for transfers between devices  26.1 us (28%)
  blocking collectives  22.3 us (24%)
  Pallas kernels  14.6 us (16%)
    all_to_all x1, waiting for transfers between devices, transpose(): lax.all_to_all(blocks, 'image', split_axis=0, concat_axis=0, tiled=True)  24.5 us
    all_to_all x1, blocking collectives, transpose(): lax.all_to_all(blocks, 'image', split_axis=0, concat_axis=0, tiled=True)  22.3 us
    all_to_all x1, starting transfers between devices, transpose(): lax.all_to_all(blocks, 'image', split_axis=0, concat_axis=0, tiled=True)  16.1 us
    pallas_call x5, Pallas kernels, call(): pl.pallas_call(kernel, out_shape=outs, in_specs=[VMEM] * len(args), out_s...  13.2 us
    ppermute x2, starting transfers between devices, slab_shift(): return lax.ppermute(array, 'space', pairs)  10.9 us
  transfers between devices with their start and end apart: 3, of which 2 were waited for; matrix products, arithmetic and copies ran while one was open for 0% of the time, Pallas kernels for 7%

profile of v5, /device:TPU:1, one launch (start us, length us, event | category | flops | bytes accessed | tf_op | source)
XLA Modules:
  0.0 92.0 jit_solution(7807728521492494928)
XLA Ops:
  0.6 0.0 copy-start.6
  0.6 0.0 copy-start.5
  0.7 0.0 copy-start.7
  0.7 0.0 copy-start.1
  0.7 1.4 %shard_map.77 = f32[32,128]{1,0:T(8,128)} custom-call(s32[64]{0:T(128)} %r_0_.2, f32[4]{0:T(128)} %r_1_.1, f32[3,64,128]{2,1,0:T(8,128)} %bitcast.21, f32[3,64,128]{2,1,0:T(8,128)} %bitcast.23, s32[64,128]{1,0:T(8,128)} %r_4_.1), custom_call_target="tpu_custom_call" | custom-call | tf_op jit(solution)/shard_map/pallas_call | solution.py:437
  2.1 0.0 copy-start
  2.1 4.7 %collective-permute-start = (f32[32,128]{1,0:T(8,128)}, f32[32,128]{1,0:T(8,128)S(1)}, u32[]{:S(2)}, u32[]{:S(2)}) collective-permute-start(f32[32,128]{1,0:T(8,128)} %shard_map.77), channel_id=1, source_target_pairs={{0,1},{1,2},{2,3},{3,4},{4,5},{5,6},{6,7},{7,8},{8,9},{9,10},{10,1... | collective-permute-start | bytes 49160 | tf_op jit(solution)/shard_map/ppermute | solution.py:395
  6.8 0.0 copy-done.6
  6.8 0.1 fusion.r_2_.r_1_
  6.9 0.0 copy-done.5
  6.9 0.0 copy-done.7
  6.9 0.1 select_reduce_fusion
  7.0 0.0 copy-done.1
  7.0 0.0 copy-done
  7.1 3.3 %shard_map.78 = (f32[576,128]{1,0:T(8,128)S(1)}, f32[576,128]{1,0:T(8,128)S(1)}) custom-call(f32[3,64,128]{2,1,0:T(8,128)S(1)} %bitcast.22, f32[3,64,128]{2,1,0:T(8,128)S(1)} %bitcast.24, f32[64,128]{1,0:T(8,128)S(1)} %fusion.r_2_.r_1_, f32[64,128]{1,0:T(8,128)S(1)} %divide_multiply_fusion.r_3_), custom_call_target="tpu_custom_call" | custom-call | flops 20000000000 | bytes 1000000 | tf_op jit(solution)/shard_map/pallas_call | solution.py:403
  10.3 1.6 %collective-permute-done.r_0_.r_1_ = f32[32,128]{1,0:T(8,128)S(1)} collective-permute-done((f32[32,128]{1,0:T(8,128)}, f32[32,128]{1,0:T(8,128)S(1)}, u32[]{:S(2)}, u32[]{:S(2)}) %collective-permute-start) | collective-permute-done | bytes 16416 | tf_op jit(solution)/shard_map/ppermute | solution.py:395
  11.9 0.0 copy-start.2
  11.9 1.4 %shard_map.79 = f32[768,128]{1,0:T(8,128)} custom-call(f32[32,128]{1,0:T(8,128)S(1)} %collective-permute-done.r_0_.r_1_, f32[64,128]{1,0:T(8,128)S(1)} %fusion.r_2_.r_1_, f32[576,128]{1,0:T(8,128)S(1)} %get-tuple-element.8.r_2_, f32[576,128]{1,0:T(8,128)S(1)} %get-tuple-element.9.r_3_), custom_call_target="tpu_custom_call" | custom-call | flops 20000000000 | bytes 1000000 | tf_op jit(solution)/shard_map/pallas_call | solution.py:403
  13.2 16.1 %all-to-all-start = ((f32[32,6,4,128]{3,2,1,0:T(4,128)}), f32[32,6,4,128]{3,2,1,0:T(4,128)S(1)}, u32[]{:S(2)}, u32[]{:S(2)}) async-start(f32[32,6,4,128]{3,2,1,0:T(4,128)} %bitcast.6), calls=%async_computation | async-start | bytes 786432 | tf_op jit(solution)/shard_map/all_to_all | solution.py:399
  29.4 0.1 pad.3.clone
  29.5 0.0 copy-done.2
  29.5 0.0 slice-start
  29.5 0.7 slice-done
  30.2 0.0 copy-start.4
  30.2 0.1 maximum_maximum_fusion.r_1_
  30.3 24.5 %all-to-all-done = f32[32,6,4,128]{3,2,1,0:T(4,128)S(1)} async-done(((f32[32,6,4,128]{3,2,1,0:T(4,128)}), f32[32,6,4,128]{3,2,1,0:T(4,128)S(1)}, u32[]{:S(2)}, u32[]{:S(2)}) %all-to-all-start) | async-done | bytes 393248 | tf_op jit(solution)/shard_map/all_to_all | solution.py:399
  54.8 0.0 copy-done.4
  54.8 4.2 %shard_map.80 = f32[384,128]{1,0:T(8,128)S(1)} custom-call(bf16[64,192]{1,0:T(8,128)(2,1)S(1)} %copy-done.4, f32[8,128]{1,0:T(8,128)S(1)} %maximum_maximum_fusion.r_1_, f32[768,128]{1,0:T(8,128)S(1)} %bitcast.17), custom_call_target="tpu_custom_call" | custom-call | flops 20000000000 | bytes 1000000 | tf_op jit(solution)/shard_map/pallas_call | solution.py:403
  59.0 22.3 %all_to_all.10 = f32[32,3,4,128]{3,2,1,0:T(4,128)S(1)} all-to-all(f32[32,3,4,128]{3,2,1,0:T(4,128)S(1)} %bitcast.20), channel_id=1, replica_groups=mesh['image'=32,'space'=16] {'image'}, dimensions={0} | all-to-all | bytes 393216 | tf_op jit(solution)/shard_map/all_to_all | solution.py:399
  81.3 0.0 copy-start.3
  81.3 6.2 %collective-permute-start.1 = (f32[16,128]{1,0:T(8,128)S(1)}, f32[16,128]{1,0:T(8,128)S(1)}, u32[]{:S(2)}, u32[]{:S(2)}) collective-permute-start(f32[16,128]{1,0:T(8,128)S(1)} %concatenate.15), channel_id=1, source_target_pairs={{0,15},{1,0},{2,1},{3,2},{4,3},{5,4},{6,5},{7,6},{8,7},{9,8},{10,9... | collective-permute-start | bytes 24584 | tf_op jit(solution)/shard_map/ppermute | solution.py:395
  87.5 0.0 copy-done.3
  87.5 3.3 %shard_map.81 = (f32[576,128]{1,0:T(8,128)S(1)}, f32[576,128]{1,0:T(8,128)S(1)}) custom-call(f32[384,128]{1,0:T(8,128)S(1)} %bitcast.19, f32[32,128]{1,0:T(8,128)S(1)} %copy-done.3, f32[64,128]{1,0:T(8,128)S(1)} %fusion.r_2_.r_1_, f32[64,128]{1,0:T(8,128)S(1)} %divide_multiply_fusion.r_3_), custom_call_target="tpu_custom_call" | custom-call | flops 20000000000 | bytes 1000000 | tf_op jit(solution)/shard_map/pallas_call | solution.py:403
  90.9 0.0 collective-permute-done.1.r_0_
  90.9 1.1 %shard_map.82 = (f32[3,64,128]{2,1,0:T(8,128)}, f32[3,64,128]{2,1,0:T(8,128)}) custom-call(f32[16,128]{1,0:T(8,128)S(1)} %collective-permute-done.1.r_0_, f32[64,128]{1,0:T(8,128)S(1)} %fusion.r_2_.r_1_, f32[576,128]{1,0:T(8,128)S(1)} %get-tuple-element.10.r_2_, f32[576,128]{1,0:T(8,128)S(1)} %get-tuple-element.11.r_3_), custom_call_target="tpu_custom_call" | custom-call | flops 20000000000 | bytes 1000000 | tf_op jit(solution)/shard_map/pallas_call | solution.py:403
  (9 shorter events, 0.1 us)
Async XLA Ops:
  0.6 6.2 %copy-start.6 = (s32[64]{0:T(128)S(1)}, s32[64]{0:T(128)}, u32[]{:S(2)}) copy-start(s32[64]{0:T(128)} %r_0_.2) | copy-start | bytes 772
  0.6 6.3 %copy-start.5 = (s32[64,128]{1,0:T(8,128)S(1)}, s32[64,128]{1,0:T(8,128)}, u32[]{:S(2)}) copy-start(s32[64,128]{1,0:T(8,128)} %r_4_.1) | copy-start | bytes 98308
  0.7 6.3 %copy-start.7 = (f32[4]{0:T(128)S(1)}, f32[4]{0:T(128)}, u32[]{:S(2)}) copy-start(f32[4]{0:T(128)} %r_1_.1) | copy-start | bytes 52
  0.7 6.4 %copy-start.1 = (f32[1,64,3,128]{3,1,2,0:T(8,128)S(1)}, f32[1,64,3,128]{3,1,2,0:T(8,128)}, u32[]{:S(2)}) copy-start(f32[1,64,3,128]{3,1,2,0:T(8,128)} %param.7) | copy-start | bytes 294916
  2.1 4.9 %copy-start = (f32[1,64,3,128]{3,1,2,0:T(8,128)S(1)}, f32[1,64,3,128]{3,1,2,0:T(8,128)}, u32[]{:S(2)}) copy-start(f32[1,64,3,128]{3,1,2,0:T(8,128)} %param.6) | copy-start | bytes 294916
  2.1 9.8 %collective-permute-start = (f32[32,128]{1,0:T(8,128)}, f32[32,128]{1,0:T(8,128)S(1)}, u32[]{:S(2)}, u32[]{:S(2)}) collective-permute-start(f32[32,128]{1,0:T(8,128)} %shard_map.77), channel_id=1, source_target_pairs={{0,1},{1,2},{2,3},{3,4},{4,5},{5,6},{6,7},{7,8},{8,9},{9,10},{10,1... | collective-permute-start | bytes 49160 | tf_op jit(solution)/shard_map/ppermute | solution.py:395
  11.9 17.6 %copy-start.2 = (f32[32,128]{1,0:T(8,128)}, f32[32,128]{1,0:T(8,128)S(1)}, u32[]{:S(2)}) copy-start(f32[32,128]{1,0:T(8,128)S(1)} %collective-permute-done.r_0_.r_1_) | copy-start | bytes 49156
  13.2 41.6 %all-to-all-start = ((f32[32,6,4,128]{3,2,1,0:T(4,128)}), f32[32,6,4,128]{3,2,1,0:T(4,128)S(1)}, u32[]{:S(2)}, u32[]{:S(2)}) async-start(f32[32,6,4,128]{3,2,1,0:T(4,128)} %bitcast.6), calls=%async_computation | async-start | bytes 786432 | tf_op jit(solution)/shard_map/all_to_all | solution.py:399
  29.5 0.7 slice-start
  30.2 24.6 %copy-start.4 = (bf16[64,192]{1,0:T(8,128)(2,1)S(1)}, bf16[64,192]{1,0:T(8,128)(2,1)}, u32[]{:S(2)}) copy-start(bf16[64,192]{1,0:T(8,128)(2,1)} %constant.49.clone.r_0_) | copy-start | bytes 73732
  81.3 6.2 %copy-start.3 = (f32[32,128]{1,0:T(8,128)S(1)}, f32[32,128]{1,0:T(8,128)}, u32[]{:S(2)}) copy-start(f32[32,128]{1,0:T(8,128)} %copy-done.2) | copy-start | bytes 49156
  81.3 9.5 %collective-permute-start.1 = (f32[16,128]{1,0:T(8,128)S(1)}, f32[16,128]{1,0:T(8,128)S(1)}, u32[]{:S(2)}, u32[]{:S(2)}) collective-permute-start(f32[16,128]{1,0:T(8,128)S(1)} %concatenate.15), channel_id=1, source_target_pairs={{0,15},{1,0},{2,1},{3,2},{4,3},{5,4},{6,5},{7,6},{8,7},{9,8},{10,9... | collective-permute-start | bytes 24584 | tf_op jit(solution)/shard_map/ppermute | solution.py:395

commit v6 on v5

--- a/solution.py
+++ b/solution.py
@@ -177,6 +177,7 @@
 
 
 VMEM = pl.BlockSpec(memory_space=pltpu.VMEM)
+SMEM = pl.BlockSpec(memory_space=pltpu.SMEM)
 PARAMS = pltpu.CompilerParams(vmem_limit_bytes=48 * 1024 * 1024)
 
 
@@ -221,8 +222,8 @@
 
 
 def first_outer_kernel(
-    cells, edge_ref, occ_ref, place_ref, speed_ref, send_ref,
-    place, speed, weights, left, right, moved,
+    cells, block_ref, edge_ref, occ_ref, kick_ref, place_ref, speed_ref, send_ref, info_ref,
+    occ_all, kick_all, place, speed, weights, left, right, moved,
 ):
     half = cells // 4
     place[32:, :] = place_ref[32:, :]
@@ -240,6 +241,17 @@
         tables, weights, [(own, own > 0, True) for own in range(4)], emit, GROUP
     )
     emit(4, force_of(tables, 4, None, carry))
+    occ_all[0:4, :] = edge_ref[24:28, :]
+    occ_all[4 : cells + 4, :] = occ_ref[...]
+    kick_all[0:3, :] = edge_ref[21:24, :]
+    kick_all[3 : cells + 3, :] = kick_ref[...]
+    start = 2 * block_ref[0] + 1
+    for near in range(4):
+        info_ref[near : near + 1, :] = occ_all[pl.ds(start + near, 1), :]
+    for near in range(2):
+        info_ref[4 + near : 5 + near, :] = kick_all[pl.ds(start + near, 1), :]
+    info_ref[6:7, :] = occ_ref[0:1, :]
+    info_ref[7:8, :] = jnp.zeros((1, LANES), F32)
     for kind, source in enumerate((place, speed)):
         for axis in range(3):
             for near in range(4):
@@ -403,7 +415,7 @@
         return pl.pallas_call(
             kernel,
             out_shape=outs,
-            in_specs=[VMEM] * len(args),
+            in_specs=[SMEM if arg.ndim == 1 else VMEM for arg in args],
             out_specs=jax.tree.map(lambda _: VMEM, outs),
             scratch_shapes=scratches,
             compiler_params=PARAMS,
@@ -433,14 +445,13 @@
     slab_scratch = [weight_scratch(cells)] + [scratch(rows * ROWS)] * 3
     edge_scratch = [scratch(rows * 8)] * 2 + [weight_scratch(8)] + [scratch(16 * ROWS)] * 3
     last = cells // 8 - 1
-    smem = pl.BlockSpec(memory_space=pltpu.SMEM)
     edge = pl.pallas_call(
         lambda *r: edge_kernel(cells, *r),
         grid=(1,),
         out_shape=shaped(32, LANES),
         in_specs=[
-            smem,
-            smem,
+            SMEM,
+            SMEM,
             pl.BlockSpec((3, 8, LANES), lambda i: (0, last, 0)),
             pl.BlockSpec((3, 8, LANES), lambda i: (0, last, 0)),
             pl.BlockSpec((8, LANES), lambda i: (last, 0)),
@@ -455,31 +466,20 @@
         slab_scratch,
         pos, vel, occupied, kick,
     )
-    send = call(
+    send, info = call(
         lambda *r: first_outer_kernel(cells, *r),
-        shaped(images * WIDE, LANES),
-        edge_scratch,
-        edge, occupied, place, speed,
+        (shaped(images * WIDE, LANES), shaped(8, LANES)),
+        [scratch(rows)] * 2 + edge_scratch,
+        block.reshape(1), edge, occupied, kick, place, speed,
     )
     got = transpose(send)
-    occ_wide = jnp.concatenate([edge[24:28], occupied], axis=0)
-    kick_wide = jnp.concatenate([edge[21:24], kick], axis=0)
-    info = jnp.concatenate(
-        [
-            lax.dynamic_slice_in_dim(occ_wide, 2 * block + 1, 4, 0),
-            lax.dynamic_slice_in_dim(kick_wide, 2 * block + 1, 2, 0),
-            occupied[0:1],
-            jnp.zeros((1, LANES), F32),
-        ],
-        axis=0,
-    )
     send = call(
         lambda *r: middle_kernel(images, *r),
         shaped(images * SPAN, LANES),
         [scratch(2 * images * 8), weight_scratch(3 * images)] + [scratch(4 * images * ROWS)] * 3,
         matrix, info, got,
     )
-    got = transpose(send)
+    got, info = lax.optimization_barrier((transpose(send), info))
     chunk = 2 * SPAN
     message = jnp.concatenate(
         [got[0:SPAN]]

time: 92.4 us -> 91.3 us (0.988)
  blocking collectives: 22.3 us -> 63.6 us
  waiting for transfers between devices: 26.1 us -> 1.54 us
  starting transfers between devices: 27 us -> 10.9 us
    all_to_all x1 -> x2, blocking collectives: 22.3 us -> 63.6 us  [transpose(): lax.all_to_all(blocks, 'image', split_axis=0, concat_axis=0, tiled=True)]
    all_to_all x1 -> x0, waiting for transfers between devices: 24.5 us -> none  [transpose(): lax.all_to_all(blocks, 'image', split_axis=0, concat_axis=0, tiled=True)]
    all_to_all x1 -> x0, starting transfers between devices: 16.1 us -> none  [transpose(): lax.all_to_all(blocks, 'image', split_axis=0, concat_axis=0, tiled=True)]
  transfers between devices with their start and end apart: 3 -> 2, of which waited for: 2 -> 1; matrix products, arithmetic and copies ran while one was open for 0% -> 0% of each run, Pallas kernels for 7% -> 7%
where the time goes in v6:
time: 91.3 us; the launch traced here: 91 us
  blocking collectives  63.6 us (70%)
  Pallas kernels  13.9 us (15%)
  starting transfers between devices  10.9 us (12%)
  waiting for transfers between devices  1.54 us (2%)
    all_to_all x2, blocking collectives, transpose(): lax.all_to_all(blocks, 'image', split_axis=0, concat_axis=0, tiled=True)  63.6 us
    pallas_call x5, Pallas kernels, call(): pl.pallas_call(kernel, out_shape=outs, in_specs=[SMEM if arg.ndim == 1 el...  12.5 us
    ppermute x2, starting transfers between devices, slab_shift(): return lax.ppermute(array, 'space', pairs)  10.9 us
  transfers between devices with their start and end apart: 2, of which 1 were waited for; matrix products, arithmetic and copies ran while one was open for 0% of the time, Pallas kernels for 7%

profile of v6, /device:TPU:1, one launch (start us, length us, event | category | flops | bytes accessed | tf_op | source)
XLA Modules:
  0.0 91.0 jit_solution(8910058098878447629)
XLA Ops:
  0.6 0.0 copy-start.4
  0.6 0.0 copy-start.3
  0.7 0.0 copy-start.5
  0.7 0.0 copy-start.1
  0.7 1.4 %shard_map.77 = f32[32,128]{1,0:T(8,128)} custom-call(s32[64]{0:T(128)} %r_0_.2, f32[4]{0:T(128)} %r_1_.1, f32[3,64,128]{2,1,0:T(8,128)} %bitcast.23, f32[3,64,128]{2,1,0:T(8,128)} %bitcast.25, s32[64,128]{1,0:T(8,128)} %r_4_.1), custom_call_target="tpu_custom_call" | custom-call | tf_op jit(solution)/shard_map/pallas_call | solution.py:448
  2.1 0.0 copy-start
  2.1 4.7 %collective-permute-start = (f32[32,128]{1,0:T(8,128)}, f32[32,128]{1,0:T(8,128)S(1)}, u32[]{:S(2)}, u32[]{:S(2)}) collective-permute-start(f32[32,128]{1,0:T(8,128)} %shard_map.77), channel_id=1, source_target_pairs={{0,1},{1,2},{2,3},{3,4},{4,5},{5,6},{6,7},{7,8},{8,9},{9,10},{10,1... | collective-permute-start | bytes 49160 | tf_op jit(solution)/shard_map/ppermute | solution.py:407
  6.8 0.0 copy-done.4
  6.8 0.1 fusion.r_2_.r_1_
  6.9 0.0 copy-done.3
  6.9 0.0 copy-done.5
  6.9 0.1 select_reduce_fusion
  7.0 0.0 copy-done.1
  7.0 0.0 copy-done
  7.1 3.3 %shard_map.78 = (f32[576,128]{1,0:T(8,128)S(1)}, f32[576,128]{1,0:T(8,128)S(1)}) custom-call(f32[3,64,128]{2,1,0:T(8,128)S(1)} %bitcast.24, f32[3,64,128]{2,1,0:T(8,128)S(1)} %bitcast.26, f32[64,128]{1,0:T(8,128)S(1)} %fusion.r_2_.r_1_, f32[64,128]{1,0:T(8,128)S(1)} %divide_multiply_fusion.r_3_), custom_call_target="tpu_custom_call" | custom-call | flops 20000000000 | bytes 1000000 | tf_op jit(solution)/shard_map/pallas_call | solution.py:415
  10.4 1.5 %collective-permute-done.r_1_ = f32[32,128]{1,0:T(8,128)S(1)} collective-permute-done((f32[32,128]{1,0:T(8,128)}, f32[32,128]{1,0:T(8,128)S(1)}, u32[]{:S(2)}, u32[]{:S(2)}) %collective-permute-start) | collective-permute-done | bytes 16416 | tf_op jit(solution)/shard_map/ppermute | solution.py:407
  11.9 0.6 shard_map.79
  12.5 0.0 copy-start.2
  12.5 41.4 %all_to_all.10 = f32[32,6,4,128]{3,2,1,0:T(4,128)S(1)} all-to-all(f32[32,6,4,128]{3,2,1,0:T(4,128)S(1)} %bitcast.17), channel_id=1, replica_groups=mesh['image'=32,'space'=16] {'image'}, dimensions={0} | all-to-all | bytes 786432 | tf_op jit(solution)/shard_map/all_to_all | solution.py:411
  53.9 0.0 copy-done.2
  53.9 4.2 %shard_map.80 = f32[384,128]{1,0:T(8,128)S(1)} custom-call(bf16[64,192]{1,0:T(8,128)(2,1)S(1)} %copy-done.2, f32[8,128]{1,0:T(8,128)S(1)} %get-tuple-element.17.r_1_, f32[768,128]{1,0:T(8,128)S(1)} %bitcast.18), custom_call_target="tpu_custom_call" | custom-call | flops 20000000000 | bytes 1000000 | tf_op jit(solution)/shard_map/pallas_call | solution.py:415
  58.1 22.3 %all_to_all.11 = f32[32,3,4,128]{3,2,1,0:T(4,128)S(1)} all-to-all(f32[32,3,4,128]{3,2,1,0:T(4,128)S(1)} %bitcast.22), channel_id=1, replica_groups=mesh['image'=32,'space'=16] {'image'}, dimensions={0} | all-to-all | bytes 393216 | tf_op jit(solution)/shard_map/all_to_all | solution.py:411
  80.4 6.2 %collective-permute-start.1 = (f32[16,128]{1,0:T(8,128)S(1)}, f32[16,128]{1,0:T(8,128)S(1)}, u32[]{:S(2)}, u32[]{:S(2)}) collective-permute-start(f32[16,128]{1,0:T(8,128)S(1)} %concatenate.3), channel_id=1, source_target_pairs={{0,15},{1,0},{2,1},{3,2},{4,3},{5,4},{6,5},{7,6},{8,7},{9,8},{10,9... | collective-permute-start | bytes 24584 | tf_op jit(solution)/shard_map/ppermute | solution.py:407
  86.6 3.3 %shard_map.81 = (f32[576,128]{1,0:T(8,128)S(1)}, f32[576,128]{1,0:T(8,128)S(1)}) custom-call(f32[384,128]{1,0:T(8,128)S(1)} %bitcast.21, f32[32,128]{1,0:T(8,128)S(1)} %collective-permute-done.r_1_, f32[64,128]{1,0:T(8,128)S(1)} %fusion.r_2_.r_1_, f32[64,128]{1,0:T(8,128)S(1)} %divide_multiply_fusion.r_3_), custom_call_target="tpu_custom_call" | custom-call | flops 20000000000 | bytes 1000000 | tf_op jit(solution)/shard_map/pallas_call | solution.py:415
  89.9 0.0 collective-permute-done.1.r_0_
  89.9 1.1 %shard_map.82 = (f32[3,64,128]{2,1,0:T(8,128)}, f32[3,64,128]{2,1,0:T(8,128)}) custom-call(f32[16,128]{1,0:T(8,128)S(1)} %collective-permute-done.1.r_0_, f32[64,128]{1,0:T(8,128)S(1)} %fusion.r_2_.r_1_, f32[576,128]{1,0:T(8,128)S(1)} %get-tuple-element.18.r_2_, f32[576,128]{1,0:T(8,128)S(1)} %get-tuple-element.19.r_3_), custom_call_target="tpu_custom_call" | custom-call | flops 20000000000 | bytes 1000000 | tf_op jit(solution)/shard_map/pallas_call | solution.py:415
  (5 shorter events, 0.0 us)
Async XLA Ops:
  0.6 6.2 %copy-start.4 = (s32[64]{0:T(128)S(1)}, s32[64]{0:T(128)}, u32[]{:S(2)}) copy-start(s32[64]{0:T(128)} %r_0_.2) | copy-start | bytes 772
  0.6 6.3 %copy-start.3 = (s32[64,128]{1,0:T(8,128)S(1)}, s32[64,128]{1,0:T(8,128)}, u32[]{:S(2)}) copy-start(s32[64,128]{1,0:T(8,128)} %r_4_.1) | copy-start | bytes 98308
  0.7 6.3 %copy-start.5 = (f32[4]{0:T(128)S(1)}, f32[4]{0:T(128)}, u32[]{:S(2)}) copy-start(f32[4]{0:T(128)} %r_1_.1) | copy-start | bytes 52
  0.7 6.4 %copy-start.1 = (f32[1,64,3,128]{3,1,2,0:T(8,128)S(1)}, f32[1,64,3,128]{3,1,2,0:T(8,128)}, u32[]{:S(2)}) copy-start(f32[1,64,3,128]{3,1,2,0:T(8,128)} %param.7) | copy-start | bytes 294916
  2.1 4.9 %copy-start = (f32[1,64,3,128]{3,1,2,0:T(8,128)S(1)}, f32[1,64,3,128]{3,1,2,0:T(8,128)}, u32[]{:S(2)}) copy-start(f32[1,64,3,128]{3,1,2,0:T(8,128)} %param.6) | copy-start | bytes 294916
  2.1 9.8 %collective-permute-start = (f32[32,128]{1,0:T(8,128)}, f32[32,128]{1,0:T(8,128)S(1)}, u32[]{:S(2)}, u32[]{:S(2)}) collective-permute-start(f32[32,128]{1,0:T(8,128)} %shard_map.77), channel_id=1, source_target_pairs={{0,1},{1,2},{2,3},{3,4},{4,5},{5,6},{6,7},{7,8},{8,9},{9,10},{10,1... | collective-permute-start | bytes 49160 | tf_op jit(solution)/shard_map/ppermute | solution.py:407
  12.5 41.4 %copy-start.2 = (bf16[64,192]{1,0:T(8,128)(2,1)S(1)}, bf16[64,192]{1,0:T(8,128)(2,1)}, u32[]{:S(2)}) copy-start(bf16[64,192]{1,0:T(8,128)(2,1)} %constant.40.clone.r_0_) | copy-start | bytes 73732
  80.4 9.5 %collective-permute-start.1 = (f32[16,128]{1,0:T(8,128)S(1)}, f32[16,128]{1,0:T(8,128)S(1)}, u32[]{:S(2)}, u32[]{:S(2)}) collective-permute-start(f32[16,128]{1,0:T(8,128)S(1)} %concatenate.3), channel_id=1, source_target_pairs={{0,15},{1,0},{2,1},{3,2},{4,3},{5,4},{6,5},{7,6},{8,7},{9,8},{10,9... | collective-permute-start | bytes 24584 | tf_op jit(solution)/shard_map/ppermute | solution.py:407

commit v7 on v6

--- a/solution.py
+++ b/solution.py
@@ -73,7 +73,7 @@
     def put_right(ref, pieces, norms):
         for axis in range(3):
             high, mid, low = pieces[axis]
-            for row, value in ((0, high), (4, high), (8, mid), (12, high), (16, low), (20, mid)):
+            for row, value in ((0, high), (4, low), (8, mid), (12, high), (16, high), (20, mid)):
                 put(ref, row + axis, value)
         for piece in range(3):
             put(ref, 8 * piece + 3, one)
@@ -85,7 +85,7 @@
         norms = norm(scaled)
         for axis in range(3):
             high, mid, low = pieces[axis]
-            for row, value in ((0, high), (4, mid), (8, high), (12, low), (16, high), (20, mid)):
+            for row, value in ((0, high), (4, high), (8, high), (12, mid), (16, low), (20, mid)):
                 put(left, row + axis, value)
         for piece in range(3):
             put(left, 8 * piece + 3, norms[piece])
@@ -120,13 +120,17 @@
     weights[index * LANES : (index + 1) * LANES, start:] = jnp.exp2(exponent).astype(BF16)
 
 
-def fold(sums):
-    return sums[0:8], sums[0:8] + sums[8:16] + sums[16:24]
+def fold(rows):
+    return rows[0:8], rows[0:8] + rows[8:16] + pltpu.roll(rows[0:8], 4, 0)
+
+
+def pieces_of(table):
+    return table[0:16].astype(BF16)
 
 
 def own_sums(tables, weights, index, own, near):
     both = jnp.concatenate(
-        [factor(table_rows(tables[1], own)), factor(table_rows(tables[2], near))], axis=1
+        [pieces_of(table_rows(tables[1], own)), pieces_of(table_rows(tables[2], near))], axis=1
     )
     weight = weights[index * LANES : (index + 1) * LANES, :]
     return fold(
@@ -138,7 +142,7 @@
     weight = weights[index * LANES : (index + 1) * LANES, LANES:]
     return fold(
         lax.dot_general(
-            factor(table_rows(tables[1], own)),
+            pieces_of(table_rows(tables[1], own)),
             weight,
             (((1,), (0,)), ((), ())),
             preferred_element_type=F32,
@@ -147,8 +151,7 @@
 
 
 def force_of(tables, own, sums, carry):
-    table = table_rows(tables[1], own)
-    place = table[0:8] + table[8:16] + table[16:24]
+    place = fold(table_rows(tables[1], own))[1]
     total = 0.0
     if sums is not None:
         total = place * sums[0][3:4] - sums[1]

time: 91.3 us -> 91 us (level)
  no operation moved by 1% of the time
where the time goes in v7:
time: 91 us; the launch traced here: 90.6 us
  blocking collectives  63.5 us (70%)
  Pallas kernels  13.5 us (15%)
  starting transfers between devices  10.9 us (12%)
  waiting for transfers between devices  1.65 us (2%)
    all_to_all x2, blocking collectives, transpose(): lax.all_to_all(blocks, 'image', split_axis=0, concat_axis=0, tiled=True)  63.5 us
    pallas_call x5, Pallas kernels, call(): pl.pallas_call(kernel, out_shape=outs, in_specs=[SMEM if arg.ndim == 1 el...  12.1 us
    ppermute x2, starting transfers between devices, slab_shift(): return lax.ppermute(array, 'space', pairs)  10.9 us
  transfers between devices with their start and end apart: 2, of which 1 were waited for; matrix products, arithmetic and copies ran while one was open for 0% of the time, Pallas kernels for 7%

profile of v7, /device:TPU:1, one launch (start us, length us, event | category | flops | bytes accessed | tf_op | source)
XLA Modules:
  0.0 90.6 jit_solution(8730069208590305305)
XLA Ops:
  0.6 0.0 copy-start.4
  0.6 0.0 copy-start.3
  0.7 0.0 copy-start.5
  0.7 0.0 copy-start.1
  0.7 1.4 %shard_map.77 = f32[32,128]{1,0:T(8,128)} custom-call(s32[64]{0:T(128)} %r_0_.2, f32[4]{0:T(128)} %r_1_.1, f32[3,64,128]{2,1,0:T(8,128)} %bitcast.23, f32[3,64,128]{2,1,0:T(8,128)} %bitcast.25, s32[64,128]{1,0:T(8,128)} %r_4_.1), custom_call_target="tpu_custom_call" | custom-call | tf_op jit(solution)/shard_map/pallas_call | solution.py:451
  2.1 0.0 copy-start
  2.1 4.7 %collective-permute-start = (f32[32,128]{1,0:T(8,128)}, f32[32,128]{1,0:T(8,128)S(1)}, u32[]{:S(2)}, u32[]{:S(2)}) collective-permute-start(f32[32,128]{1,0:T(8,128)} %shard_map.77), channel_id=1, source_target_pairs={{0,1},{1,2},{2,3},{3,4},{4,5},{5,6},{6,7},{7,8},{8,9},{9,10},{10,1... | collective-permute-start | bytes 49160 | tf_op jit(solution)/shard_map/ppermute | solution.py:410
  6.8 0.0 copy-done.4
  6.8 0.1 fusion.r_2_.r_1_
  6.9 0.0 copy-done.3
  6.9 0.0 copy-done.5
  6.9 0.1 select_reduce_fusion
  7.0 0.0 copy-done.1
  7.0 0.0 copy-done
  7.1 3.2 %shard_map.78 = (f32[576,128]{1,0:T(8,128)S(1)}, f32[576,128]{1,0:T(8,128)S(1)}) custom-call(f32[3,64,128]{2,1,0:T(8,128)S(1)} %bitcast.24, f32[3,64,128]{2,1,0:T(8,128)S(1)} %bitcast.26, f32[64,128]{1,0:T(8,128)S(1)} %fusion.r_2_.r_1_, f32[64,128]{1,0:T(8,128)S(1)} %divide_multiply_fusion.r_3_), custom_call_target="tpu_custom_call" | custom-call | flops 20000000000 | bytes 1000000 | tf_op jit(solution)/shard_map/pallas_call | solution.py:418
  10.2 1.6 %collective-permute-done.r_1_ = f32[32,128]{1,0:T(8,128)S(1)} collective-permute-done((f32[32,128]{1,0:T(8,128)}, f32[32,128]{1,0:T(8,128)S(1)}, u32[]{:S(2)}, u32[]{:S(2)}) %collective-permute-start) | collective-permute-done | bytes 16416 | tf_op jit(solution)/shard_map/ppermute | solution.py:410
  11.9 0.6 shard_map.79
  12.5 0.0 copy-start.2
  12.5 41.6 %all_to_all.10 = f32[32,6,4,128]{3,2,1,0:T(4,128)S(1)} all-to-all(f32[32,6,4,128]{3,2,1,0:T(4,128)S(1)} %bitcast.17), channel_id=1, replica_groups=mesh['image'=32,'space'=16] {'image'}, dimensions={0} | all-to-all | bytes 786432 | tf_op jit(solution)/shard_map/all_to_all | solution.py:414
  54.1 0.0 copy-done.2
  54.1 4.1 %shard_map.80 = f32[384,128]{1,0:T(8,128)S(1)} custom-call(bf16[64,192]{1,0:T(8,128)(2,1)S(1)} %copy-done.2, f32[8,128]{1,0:T(8,128)S(1)} %get-tuple-element.17.r_1_, f32[768,128]{1,0:T(8,128)S(1)} %bitcast.18), custom_call_target="tpu_custom_call" | custom-call | flops 20000000000 | bytes 1000000 | tf_op jit(solution)/shard_map/pallas_call | solution.py:418
  58.2 21.9 %all_to_all.11 = f32[32,3,4,128]{3,2,1,0:T(4,128)S(1)} all-to-all(f32[32,3,4,128]{3,2,1,0:T(4,128)S(1)} %bitcast.22), channel_id=1, replica_groups=mesh['image'=32,'space'=16] {'image'}, dimensions={0} | all-to-all | bytes 393216 | tf_op jit(solution)/shard_map/all_to_all | solution.py:414
  80.2 6.2 %collective-permute-start.1 = (f32[16,128]{1,0:T(8,128)S(1)}, f32[16,128]{1,0:T(8,128)S(1)}, u32[]{:S(2)}, u32[]{:S(2)}) collective-permute-start(f32[16,128]{1,0:T(8,128)S(1)} %concatenate.3), channel_id=1, source_target_pairs={{0,15},{1,0},{2,1},{3,2},{4,3},{5,4},{6,5},{7,6},{8,7},{9,8},{10,9... | collective-permute-start | bytes 24584 | tf_op jit(solution)/shard_map/ppermute | solution.py:410
  86.4 3.1 %shard_map.81 = (f32[576,128]{1,0:T(8,128)S(1)}, f32[576,128]{1,0:T(8,128)S(1)}) custom-call(f32[384,128]{1,0:T(8,128)S(1)} %bitcast.21, f32[32,128]{1,0:T(8,128)S(1)} %collective-permute-done.r_1_, f32[64,128]{1,0:T(8,128)S(1)} %fusion.r_2_.r_1_, f32[64,128]{1,0:T(8,128)S(1)} %divide_multiply_fusion.r_3_), custom_call_target="tpu_custom_call" | custom-call | flops 20000000000 | bytes 1000000 | tf_op jit(solution)/shard_map/pallas_call | solution.py:418
  89.5 0.0 collective-permute-done.1.r_0_
  89.5 1.1 %shard_map.82 = (f32[3,64,128]{2,1,0:T(8,128)}, f32[3,64,128]{2,1,0:T(8,128)}) custom-call(f32[16,128]{1,0:T(8,128)S(1)} %collective-permute-done.1.r_0_, f32[64,128]{1,0:T(8,128)S(1)} %fusion.r_2_.r_1_, f32[576,128]{1,0:T(8,128)S(1)} %get-tuple-element.18.r_2_, f32[576,128]{1,0:T(8,128)S(1)} %get-tuple-element.19.r_3_), custom_call_target="tpu_custom_call" | custom-call | flops 20000000000 | bytes 1000000 | tf_op jit(solution)/shard_map/pallas_call | solution.py:418
  (5 shorter events, 0.0 us)
Async XLA Ops:
  0.6 6.2 %copy-start.4 = (s32[64]{0:T(128)S(1)}, s32[64]{0:T(128)}, u32[]{:S(2)}) copy-start(s32[64]{0:T(128)} %r_0_.2) | copy-start | bytes 772
  0.6 6.3 %copy-start.3 = (s32[64,128]{1,0:T(8,128)S(1)}, s32[64,128]{1,0:T(8,128)}, u32[]{:S(2)}) copy-start(s32[64,128]{1,0:T(8,128)} %r_4_.1) | copy-start | bytes 98308
  0.7 6.3 %copy-start.5 = (f32[4]{0:T(128)S(1)}, f32[4]{0:T(128)}, u32[]{:S(2)}) copy-start(f32[4]{0:T(128)} %r_1_.1) | copy-start | bytes 52
  0.7 6.4 %copy-start.1 = (f32[1,64,3,128]{3,1,2,0:T(8,128)S(1)}, f32[1,64,3,128]{3,1,2,0:T(8,128)}, u32[]{:S(2)}) copy-start(f32[1,64,3,128]{3,1,2,0:T(8,128)} %param.7) | copy-start | bytes 294916
  2.1 4.9 %copy-start = (f32[1,64,3,128]{3,1,2,0:T(8,128)S(1)}, f32[1,64,3,128]{3,1,2,0:T(8,128)}, u32[]{:S(2)}) copy-start(f32[1,64,3,128]{3,1,2,0:T(8,128)} %param.6) | copy-start | bytes 294916
  2.1 9.8 %collective-permute-start = (f32[32,128]{1,0:T(8,128)}, f32[32,128]{1,0:T(8,128)S(1)}, u32[]{:S(2)}, u32[]{:S(2)}) collective-permute-start(f32[32,128]{1,0:T(8,128)} %shard_map.77), channel_id=1, source_target_pairs={{0,1},{1,2},{2,3},{3,4},{4,5},{5,6},{6,7},{7,8},{8,9},{9,10},{10,1... | collective-permute-start | bytes 49160 | tf_op jit(solution)/shard_map/ppermute | solution.py:410
  12.5 41.6 %copy-start.2 = (bf16[64,192]{1,0:T(8,128)(2,1)S(1)}, bf16[64,192]{1,0:T(8,128)(2,1)}, u32[]{:S(2)}) copy-start(bf16[64,192]{1,0:T(8,128)(2,1)} %constant.40.clone.r_0_) | copy-start | bytes 73732
  80.2 9.3 %collective-permute-start.1 = (f32[16,128]{1,0:T(8,128)S(1)}, f32[16,128]{1,0:T(8,128)S(1)}, u32[]{:S(2)}, u32[]{:S(2)}) collective-permute-start(f32[16,128]{1,0:T(8,128)S(1)} %concatenate.3), channel_id=1, source_target_pairs={{0,15},{1,0},{2,1},{3,2},{4,3},{5,4},{6,5},{7,6},{8,7},{9,8},{10,9... | collective-permute-start | bytes 24584 | tf_op jit(solution)/shard_map/ppermute | solution.py:410
